TPU v7x, 32 devices: a whole 2x2x4 slice. The times are simulated.
32 devices in a mesh: section: 2 (over y), dp: 16 (over z, x, core).
Axes of the slice: x: 2, y: 2, z: 4, core: 2. Of those that a mesh axis runs over, the one named last changes fastest.
Arguments:
- boundary: bfloat16 [2, 4, 19840, 512], P('section', None, 'dp'), may hold values from -6 to 6
- entry_gain: float32 [2, 512], P('section'), may hold values from 0.25 to 1.75
- entry_shift: float32 [2, 512], P('section'), may hold values from -1.75 to 1.75
- widen_weight: bfloat16 [2, 512, 3072], P('section'), may hold values from -0.25 to 0.25
- hidden_bias: float32 [2, 3072], P('section'), may hold values from -1.75 to 1.75
- gate_gain: float32 [2, 1536], P('section'), may hold values from 0.25 to 1.75
- gate_shift: float32 [2, 1536], P('section'), may hold values from -1.75 to 1.75
- spatial_weight: bfloat16 [2, 324, 324], P('section'), may hold values from -0.4375 to 0.4375
- position_bias: float32 [2, 324], P('section'), may hold values from 0.5 to 1.5
- narrow_weight: bfloat16 [2, 1536, 512], P('section'), may hold values from -0.15625 to 0.15625
- output_bias: float32 [2, 512], P('section'), may hold values from -1.75 to 1.75
- crop_starts: int32 [2, 3], P('section'), may hold values from 0 to 224, as said below
Outputs:
- results: float32 [2, 4, 19840, 512], P('section', None, 'dp')
- entry_grads: float32 [2, 3, 512], P('section')
- widen_grad: float32 [2, 512, 3072], P('section')
- hidden_grads: float32 [2, 3072], P('section')
- gate_grads: float32 [2, 2, 1536], P('section')
- spatial_grad: float32 [2, 324, 324], P('section')
- position_grads: float32 [2, 324], P('section')
- narrow_grad: float32 [2, 1536, 512], P('section')
Inputs may be any that keep to these rules, and one draw needn't show every extreme that they name: `crop_starts`: row l holds the starts of layer l's crops for images of 100, 196 and 324 patches; each crop lies inside the 324 x 324 weight, so the last start is 0.
All inputs are finite; a program needn't handle non-finite values.
Results may differ from a plain program's by a relative error of at most 0.01.
Values may be sent and summed in bfloat16 or wider, within the bound.
A program may use at most 448 MiB of HBM per device.

v0:
```python
from functools import partial

import jax
import jax.numpy as jnp
from jax import lax
from jax.sharding import PartitionSpec as P

P_SMALL = 100
P_MID = 196
P_LARGE = 324
SETS = 2


EPSILON = 1e-05


def from_behind(x, axis, by):
    peers = lax.axis_size(axis)
    pairs = [(i, i + by) for i in range(peers) if 0 <= i + by < peers]
    return lax.ppermute(x, axis, pairs)


def norm_rows(values, gain, shift):
    average = jnp.mean(values, axis=-1, keepdims=True)
    centred = values - average
    spread = jnp.mean(centred * centred, axis=-1, keepdims=True)
    return centred * lax.rsqrt(spread + EPSILON) * gain + shift


def smooth_gate(values):
    return (
        0.5
        * values
        * (1.0 + jnp.tanh(0.7978845608028654 * (values + 0.044715 * values * values * values)))
    )


def gate_piece(hidden, gain, shift):
    half = hidden.shape[-1] // 2
    active = smooth_gate(hidden)
    return (active[:, :half], norm_rows(active[:, half:], gain, shift))


def image_blocks(rows, count, first):
    return rows[first : first + SETS * count].reshape(SETS, count, rows.shape[-1])


def spatial_forward(gated, weight, bias, starts):
    pieces = []
    first = 0
    for index, count in enumerate((P_SMALL, P_MID, P_LARGE)):
        offset = starts[index]
        square = lax.dynamic_slice(weight, (offset, offset), (count, count))
        shift = lax.dynamic_slice(bias, (offset,), (count,))
        mixed = jnp.einsum(
            "pq,sqc->spc",
            square,
            image_blocks(gated, count, first),
            preferred_element_type=jnp.float32,
        )
        pieces.append((mixed + shift[None, :, None]).reshape(SETS * count, gated.shape[-1]))
        first = first + SETS * count
    return jnp.concatenate(pieces, axis=0)


def spatial_backward(gated, grad_mixed, weight, starts, weight_total, bias_total):
    pieces = []
    first = 0
    for index, count in enumerate((P_SMALL, P_MID, P_LARGE)):
        offset = starts[index]
        square = lax.dynamic_slice(weight, (offset, offset), (count, count))
        block = image_blocks(gated, count, first)
        grad_block = image_blocks(grad_mixed, count, first)
        moved = jnp.einsum("pq,spc->sqc", square, grad_block, preferred_element_type=jnp.float32)
        pieces.append(moved.reshape(SETS * count, gated.shape[-1]))
        weight_term = jnp.einsum(
            "spc,sqc->pq", grad_block, block, preferred_element_type=jnp.float32
        )
        bias_term = jnp.sum(grad_block, axis=(0, 2), dtype=jnp.float32)
        current = lax.dynamic_slice(weight_total, (offset, offset), (count, count))
        weight_total = lax.dynamic_update_slice(
            weight_total, current + weight_term, (offset, offset)
        )
        current_bias = lax.dynamic_slice(bias_total, (offset,), (count,))
        bias_total = lax.dynamic_update_slice(bias_total, current_bias + bias_term, (offset,))
        first = first + SETS * count
    return (jnp.concatenate(pieces, axis=0), weight_total, bias_total)


def layer_forward(inputs, params, starts):
    (
        entry_gain,
        entry_shift,
        widen,
        hidden_bias,
        gate_gain,
        gate_shift,
        spatial,
        position,
        narrow,
        output_bias,
    ) = params
    normed = norm_rows(inputs, entry_gain, entry_shift).astype(jnp.bfloat16)
    hidden = jnp.dot(normed, widen, preferred_element_type=jnp.float32) + hidden_bias
    upper, lower = gate_piece(hidden, gate_gain, gate_shift)
    gated = lower.astype(jnp.bfloat16)
    mixed = spatial_forward(gated, spatial, position, starts)
    product = (upper * mixed).astype(jnp.bfloat16)
    outputs = inputs + (jnp.dot(product, narrow, preferred_element_type=jnp.float32) + output_bias)
    return (outputs, (inputs, normed, hidden, gated, mixed, product))


def layer_backward(kept, grad_out, params, starts):
    inputs, normed, hidden, gated, mixed, product = kept
    (
        entry_gain,
        entry_shift,
        widen,
        hidden_bias,
        gate_gain,
        gate_shift,
        spatial,
        position,
        narrow,
        output_bias,
    ) = params
    grad_branch = grad_out.astype(jnp.bfloat16)
    grad_output_bias = jnp.sum(grad_branch, axis=0, dtype=jnp.float32)
    grad_narrow = jnp.einsum("rc,rd->cd", product, grad_branch, preferred_element_type=jnp.float32)
    grad_product = jnp.einsum("rd,cd->rc", grad_branch, narrow, preferred_element_type=jnp.float32)
    gate_values, pull_gate = jax.vjp(gate_piece, hidden, gate_gain, gate_shift)
    grad_mixed = (grad_product * gate_values[0]).astype(jnp.bfloat16)
    grad_gated, grad_spatial, grad_position = spatial_backward(
        gated,
        grad_mixed,
        spatial,
        starts,
        jnp.zeros(spatial.shape, jnp.float32),
        jnp.zeros(position.shape, jnp.float32),
    )
    grad_hidden, grad_gate_gain, grad_gate_shift = pull_gate((grad_product * mixed, grad_gated))
    grad_hidden = grad_hidden.astype(jnp.bfloat16)
    grad_hidden_bias = jnp.sum(grad_hidden, axis=0, dtype=jnp.float32)
    grad_widen = jnp.einsum("rd,rf->df", normed, grad_hidden, preferred_element_type=jnp.float32)
    grad_normed = jnp.einsum("rf,df->rd", grad_hidden, widen, preferred_element_type=jnp.float32)
    entry_values, pull_entry = jax.vjp(norm_rows, inputs, entry_gain, entry_shift)
    grad_rows, grad_entry_gain, grad_entry_shift = pull_entry(grad_normed)
    grads = (
        grad_entry_gain,
        grad_entry_shift,
        grad_widen,
        grad_hidden_bias,
        grad_gate_gain,
        grad_gate_shift,
        grad_spatial,
        grad_position,
        grad_narrow,
        grad_output_bias,
    )
    return (grad_out + grad_rows, grads)


def choose(flag, first, second):
    return jnp.where(flag, first, second)


def shards(
    boundary,
    entry_gain,
    entry_shift,
    widen_weight,
    hidden_bias,
    gate_gain,
    gate_shift,
    spatial_weight,
    position_bias,
    narrow_weight,
    output_bias,
    crop_starts,
):
    params = tuple(
        (
            item[0]
            for item in (
                entry_gain,
                entry_shift,
                widen_weight,
                hidden_bias,
                gate_gain,
                gate_shift,
                spatial_weight,
                position_bias,
                narrow_weight,
                output_bias,
            )
        )
    )
    starts = crop_starts[0]
    first_section = lax.axis_index("section") == 0
    sources = boundary[0]
    micro = sources.shape[0]
    zero_rows = jnp.zeros(sources.shape[1:], jnp.bfloat16)
    received = zero_rows
    returned = zero_rows
    totals = tuple((jnp.zeros(item.shape, jnp.float32) for item in params))
    kept_ticks = {}
    outputs_by_tick = {}
    grads_by_tick = {}
    for tick in range(micro + 2):
        if tick <= micro:
            start_rows = jnp.where(first_section, sources[min(tick, micro - 1)], received).astype(
                jnp.float32
            )
            outputs, kept = layer_forward(start_rows, params, starts)
            kept_ticks[tick] = kept
            outputs_by_tick[tick] = outputs
            if tick < micro:
                received = from_behind(outputs.astype(jnp.bfloat16), "section", 1)
        if tick >= 1:
            earlier = max(tick - 2, 0)
            later = min(tick, micro)
            used = jax.tree.map(
                partial(choose, first_section), kept_ticks[earlier], kept_ticks[later]
            )
            grad_out = jnp.where(first_section, returned, sources[min(tick - 1, micro - 1)]).astype(
                jnp.float32
            )
            grad_rows, grads = layer_backward(used, grad_out, params, starts)
            valid = jnp.where(first_section, tick >= 2, tick <= micro)
            grads = tuple((jnp.where(valid, item, 0.0) for item in grads))
            grads_by_tick[tick] = grad_rows
            if tick <= micro:
                returned = from_behind(grad_rows.astype(jnp.bfloat16), "section", -1)
            totals = tuple((left + right for left, right in zip(totals, grads)))
    summed = lax.psum(
        (
            totals[0],
            totals[1],
            totals[2],
            totals[3],
            totals[4],
            totals[5],
            totals[6],
            totals[7],
            totals[8],
            totals[9],
        ),
        "dp",
    )
    rows_out = []
    for index in range(micro):
        rows_out.append(
            jnp.where(first_section, grads_by_tick[index + 2], outputs_by_tick[index + 1])
        )
    results = jnp.stack(rows_out)[None]
    entry_grads = jnp.stack([summed[0], summed[1], summed[9]])[None]
    gate_grads = jnp.stack([summed[4], summed[5]])[None]
    return (
        results,
        entry_grads,
        summed[2][None],
        summed[3][None],
        gate_grads,
        summed[6][None],
        summed[7][None],
        summed[8][None],
    )


def solution(mesh):
    placed = (
        P("section", None, "dp", None),
        P("section", None),
        P("section", None),
        P("section", None, None),
        P("section", None),
        P("section", None),
        P("section", None),
        P("section", None, None),
        P("section", None),
        P("section", None, None),
        P("section", None),
        P("section", None),
    )
    return jax.shard_map(
        shards,
        mesh=mesh,
        in_specs=placed,
        out_specs=(
            P("section", None, "dp", None),
            P("section", None, None),
            P("section", None, None),
            P("section", None),
            P("section", None, None),
            P("section", None, None),
            P("section", None),
            P("section", None, None),
        ),
        check_vma=False,
    )
```

profile of v0, /device:TPU:0, one launch (start us, length us, event | category | flops | bytes accessed | tf_op | source)
XLA Modules:
  0.0 1598.6 jit_solution(9403795421990876982)
XLA Ops:
  16.3 11.9 fusion.23
  94.1 26.4 %collective-permute-done = bf16[1240,512]{1,0:T(8,128)(2,1)} collective-permute-done((bf16[1240,512]{1,0:T(8,128)(2,1)}, bf16[1240,512]{1,0:T(8,128)(2,1)}, u32[]{:S(2)}, u32[]{:S(2)}) %collective-permute-start) | collective-permute-done | bytes 1269792 | tf_op jit(solution)/shard_map/ppermute | solution.py:20
  125.2 23.4 %add_multiply_fusion.4 = (f32[1240,3072]{1,0:T(8,128)}, f32[1240,3072]{1,0:T(8,128)}, f32[1240,3072]{1,0:T(8,128)}) fusion(f32[1240,3072]{1,0:T(8,128)} %get-tuple-element.170, f32[3072]{0:T(1024)S(1)} %bitcast.543, pred[]{:T(512)S(6)} %eq.3, bf16[1,512,3072]{2,1,0:T(8,128)(2,1)S(1)} %copy-done, bf16[1240,512]{1,0:T(8,128)(2,1)S(1)} %get-tuple-element.132, ...), kind=kOutput, calls=%fused_computation.84 | convolution fusion | flops 3976888320 | bytes 65390272 | tf_op jit(solution)/shard_map/dot_general | solution.py:104
  212.1 21.0 %multiply_reduce_fusion.18 = (f32[1240]{0:T(1024)S(1)}, bf16[1240,1536]{1,0:T(8,128)(2,1)}, f32[1240,1536]{1,0:T(8,128)}, bf16[1240,1536]{1,0:T(8,128)(2,1)}) fusion(f32[1240,3072]{1,0:T(8,128)} %get-tuple-element.138, f32[1240]{0:T(1024)S(1)} %broadcast_multiply_fusion.8, f32[1240,1536]{1,0:T(8,128)} %copy-done.3, ...), kind=kOutput, calls=%fused_computation.143 | convolution fusion | flops 1968126720 | bytes 56183488 | tf_op jit(solution)/shard_map/rd,cd->rc/dot_general | solution.py:130
  321.1 14.9 fusion.35
  444.3 57.2 %convert_reduce_fusion.4 = (f32[3072]{0:T(1024)}, bf16[1240,3072]{1,0:T(8,128)(2,1)}, f32[1240,3072]{1,0:T(8,128)}, f32[1240,3072]{1,0:T(8,128)}, f32[1240,3072]{1,0:T(8,128)}, /*index=5*/f32[1240,3072]{1,0:T(8,128)}) fusion(f32[1240,1536]{1,0:T(8,128)} %get-tuple-element.150, f32[1240,1536]{1,0:T(8,128)} %broadcast_add_fusion.4, ...), kind=kOutput, calls=%fused_computation.79 | convolution fusion | flops 4125447168 | bytes 133969600 | tf_op jit(solution)/shard_map/dot_general | solution.py:104
  595.3 10.9 fusion.201
  606.2 14.0 collective-permute-done.6
  634.5 25.2 %collective-permute-done.1 = bf16[1240,512]{1,0:T(8,128)(2,1)S(1)} collective-permute-done((bf16[1240,512]{1,0:T(8,128)(2,1)S(1)}, bf16[1240,512]{1,0:T(8,128)(2,1)S(1)}, u32[]{:S(2)}, u32[]{:S(2)}) %collective-permute-start.1) | collective-permute-done | bytes 1269792 | tf_op jit(solution)/shard_map/ppermute | solution.py:20
  662.3 13.8 multiply_reduce_fusion.15
  749.4 37.7 %convert_reduce_fusion.3 = (f32[3072]{0:T(1024)}, bf16[1240,3072]{1,0:T(8,128)(2,1)}, f32[1240,3072]{1,0:T(8,128)}, f32[1240,3072]{1,0:T(8,128)}) fusion(f32[1240,1536]{1,0:T(8,128)} %get-tuple-element.152, f32[1240,1536]{1,0:T(8,128)} %broadcast_add_fusion.3, f32[1240,3072]{1,0:T(8,128)} %get-tuple-element.175, f32[1240,3072]{1,0:T(8,128)} %get-tuple-element.170, ...), kind=kOutput, calls=%fused_computation.78 | convolution fusion | flops 4056880128 | bytes 88258240 | tf_op jit(solution)/shard_map/dot_general | solution.py:104
  812.8 11.2 fusion.199
  824.0 10.0 collective-permute-done.3
  840.8 13.8 multiply_reduce_fusion.12
  915.0 39.9 %convert_reduce_fusion.2 = (f32[3072]{0:T(1024)}, bf16[1240,3072]{1,0:T(8,128)(2,1)}, f32[1240,3072]{1,0:T(8,128)}, f32[1240,3072]{1,0:T(8,128)}) fusion(f32[1240,1536]{1,0:T(8,128)} %get-tuple-element.153, f32[1240,1536]{1,0:T(8,128)} %broadcast_add_fusion.2, f32[1240,3072]{1,0:T(8,128)} %get-tuple-element.178, f32[1240,3072]{1,0:T(8,128)} %get-tuple-element.171, ...), kind=kLoop, calls=%fused_computation.77 | loop fusion | flops 182842368 | bytes 99065856 | tf_op jit(solution)/shard_map/reduce_sum | solution.py:143
  1066.4 10.7 fusion.197
  1080.8 20.6 %multiply_reduce_fusion.9 = (f32[1240]{0:T(1024)S(1)}, bf16[1240,1536]{1,0:T(8,128)(2,1)}, f32[1240,1536]{1,0:T(8,128)}, bf16[1240,1536]{1,0:T(8,128)(2,1)}) fusion(f32[1240,3072]{1,0:T(8,128)} %get-tuple-element.134, f32[1240]{0:T(1024)S(1)} %copy-done.96, f32[1240,1536]{1,0:T(8,128)} %copy-done.4, f32[1240,1536]{1,0:T(8,128)} %constant_dynamic-update-slice_fusion.24, ...), kind=kOutput, calls=%fused_computation.128 | convolution fusion | flops 1967491840 | bytes 56182464 | tf_op jit(solution)/shard_map/rd,cd->rc/dot_general | solution.py:130
  1183.7 19.6 %convert_reduce_fusion.1 = (f32[3072]{0:T(1024)S(1)}, bf16[1240,3072]{1,0:T(8,128)(2,1)}) fusion(f32[1240,1536]{1,0:T(8,128)} %get-tuple-element.154, f32[1240,1536]{1,0:T(8,128)} %broadcast_add_fusion.1, f32[1240,3072]{1,0:T(8,128)S(1)} %bitcast.508, f32[1240,3072]{1,0:T(8,128)} %get-tuple-element.175, f32[3072]{0:T(1024)S(1)} %bitcast.548, pred[]{:T(512)S(6)} %eq.3), kind=kLoop, calls=%fused_computation.76 | loop fusion | flops 114275328 | bytes 53354496 | tf_op jit(solution)/shard_map/reduce_sum | solution.py:143
  1222.9 10.9 fusion.195
  1250.3 12.9 multiply_reduce_fusion.6
  1339.2 19.9 %convert_reduce_fusion = (f32[3072]{0:T(1024)S(1)}, bf16[1240,3072]{1,0:T(8,128)(2,1)}) fusion(f32[1240,1536]{1,0:T(8,128)} %get-tuple-element.156, f32[1240,1536]{1,0:T(8,128)} %broadcast_add_fusion, f32[1240,3072]{1,0:T(8,128)S(1)} %bitcast.510, f32[1240,3072]{1,0:T(8,128)} %get-tuple-element.178, f32[3072]{0:T(1024)S(1)} %bitcast.549, pred[]{:T(512)S(6)} %eq.3), kind=kLoop, calls=%fused_computation.75 | loop fusion | flops 114275328 | bytes 53354496 | tf_op jit(solution)/shard_map/reduce_sum | solution.py:143
  1371.8 13.7 add_bitcast_fusion
  1397.6 62.2 %all-reduce.10 = (f32[1,512]{1,0:T(1,128)S(1)}, f32[1,512]{1,0:T(1,128)S(1)}, f32[1,512]{1,0:T(1,128)S(1)}, f32[1,3072]{1,0:T(1,128)}, f32[1,1536]{1,0:T(1,128)S...) all-reduce(f32[1,512]{1,0:T(1,128)S(1)} %bitcast.577, ...), channel_id=1, replica_groups=mesh['section'=2,'dp'=16] {'dp'}, use_global_device_ids=true, to_apply=%region_77.78 | all-reduce | flops 8004 | bytes 64032 | tf_op jit(solution)/shard_map/psum | solution.py:235
  1473.4 107.5 %all-reduce.14.cloned.1.call-done = (f32[1,512,3072]{2,1,0:T(8,128)}, f32[1,324,324]{2,1,0:T(8,128)}, f32[1,1536,512]{2,1,0:T(8,128)}) async-done(((f32[1,512,3072]{2,1,0:T(8,128)}, f32[1,324,324]{2,1,0:T(8,128)}, f32[1,1536,512]{2,1,0:T(8,128)}), (f32[1,512,3072]{2,1,0:T(8,128)}, f32[1,324,324]{2,1,0:T(8,128)}, f32[1,1536,512]{2,1,0:T(8,128)})) %all-reduce.14.cloned.1.call-update) | async-done | bytes 9857104 | tf_op jit(solution)/shard_map/psum | solution.py:235
  (942 shorter events, 967.9 us)
Async XLA Ops:
  7.2 1573.7 %all-reduce.14.cloned.1.call-start = ((), (), s32[]{:S(2)}) async-start(), calls=%async_computation | async-start | bytes 19881984 | tf_op jit(solution)/shard_map/psum | solution.py:235
  12.0 725.7 %copy-start.87 = (f32[1536]{0:T(1024)}, f32[1536]{0:T(1024)S(1)}, u32[]{:S(2)}) copy-start(f32[1536]{0:T(1024)S(1)} %reduce.76) | copy-start | bytes 18436
  12.7 497.1 %copy-start.92 = (f32[1536]{0:T(1024)}, f32[1536]{0:T(1024)S(1)}, u32[]{:S(2)}) copy-start(f32[1536]{0:T(1024)S(1)} %reduce.77) | copy-start | bytes 18436
  38.7 522.4 %copy-start.94 = (f32[324]{0:T(512)}, f32[324]{0:T(512)S(1)}, u32[]{:S(2)}) copy-start(f32[324]{0:T(512)S(1)} %reduce.78) | copy-start | bytes 3892
  39.5 498.4 %copy-start.148 = (f32[100]{0:T(128)}, f32[100]{0:T(128)S(1)}, u32[]{:S(2)}) copy-start(f32[100]{0:T(128)S(1)} %fusion.284) | copy-start | bytes 1204
  40.2 511.1 %copy-start.101 = (f32[1,196]{1,0:T(1,128)}, f32[1,196]{1,0:T(1,128)S(1)}, u32[]{:S(2)}) copy-start(f32[1,196]{1,0:T(1,128)S(1)} %constant_dynamic-slice_fusion) | copy-start | bytes 2356
  88.0 37.2 %copy-start.98 = (f32[1,3072]{1,0:T(1,128)S(1)}, f32[1,3072]{1,0:T(1,128)}, u32[]{:S(2)}) copy-start(f32[1,3072]{1,0:T(1,128)} %param.16) | copy-start | bytes 36868
  88.0 37.2 %copy-start.99 = (f32[1,512]{1,0:T(1,128)S(1)}, f32[1,512]{1,0:T(1,128)}, u32[]{:S(2)}) copy-start(f32[1,512]{1,0:T(1,128)} %param.13) | copy-start | bytes 6148
  88.0 37.2 %copy-start.195 = (f32[1,512]{1,0:T(1,128)S(1)}, f32[1,512]{1,0:T(1,128)}, u32[]{:S(2)}) copy-start(f32[1,512]{1,0:T(1,128)} %param.14) | copy-start | bytes 6148
  88.0 32.5 %collective-permute-start = (bf16[1240,512]{1,0:T(8,128)(2,1)}, bf16[1240,512]{1,0:T(8,128)(2,1)}, u32[]{:S(2)}, u32[]{:S(2)}) collective-permute-start(bf16[1240,512]{1,0:T(8,128)(2,1)} %fusion.127), channel_id=1, source_target_pairs={{0,16},{1,17},{2,18},{3,19},{4,20},{5,21},{6,22},{7,23},{8,24},{9,... | collective-permute-start | bytes 3809288 | tf_op jit(solution)/shard_map/ppermute | solution.py:20
  286.7 30.8 %collective-permute-start.2 = (bf16[1240,512]{1,0:T(8,128)(2,1)}, bf16[1240,512]{1,0:T(8,128)(2,1)}, u32[]{:S(2)}, u32[]{:S(2)}) collective-permute-start(bf16[1240,512]{1,0:T(8,128)(2,1)} %get-tuple-element.172), channel_id=1, source_target_pairs={{0,16},{1,17},{2,18},{3,19},{4,20},{5,21},{6,22},{7,23},{8,24},{9,... | collective-permute-start | bytes 3809288 | tf_op jit(solution)/shard_map/ppermute | solution.py:20
  310.6 33.0 %slice-start.8 = ((s8[15237120]{0:T(1024)(128)(4,1)}), s8[4194304]{0:T(1024)(128)(4,1)S(1)}, s32[]{:S(2)}) async-start(s8[15237120]{0:T(1024)(128)(4,1)} %bitcast.511), calls=%async_computation.9 | async-start | bytes 8388608
  404.1 34.7 %collective-permute-start.4 = (bf16[1240,512]{1,0:T(8,128)(2,1)}, bf16[1240,512]{1,0:T(8,128)(2,1)}, u32[]{:S(2)}, u32[]{:S(2)}) collective-permute-start(bf16[1240,512]{1,0:T(8,128)(2,1)} %get-tuple-element.176), channel_id=1, source_target_pairs={{0,16},{1,17},{2,18},{3,19},{4,20},{5,21},{6,22},{7,23},{8,24},{9,... | collective-permute-start | bytes 3809288 | tf_op jit(solution)/shard_map/ppermute | solution.py:20
  440.7 60.8 %copy-start.119 = (f32[1240]{0:T(1024)}, f32[1240]{0:T(1024)S(1)}, u32[]{:S(2)}) copy-start(f32[1240]{0:T(1024)S(1)} %broadcast_multiply_fusion.14) | copy-start | bytes 14884
  444.3 57.2 %copy-start.158 = (f32[1240]{0:T(1024)}, f32[1240]{0:T(1024)S(1)}, u32[]{:S(2)}) copy-start(f32[1240]{0:T(1024)S(1)} %add_rsqrt_fusion.3) | copy-start | bytes 14884
  529.2 92.0 %copy-start.139 = (f32[1240]{0:T(1024)}, f32[1240]{0:T(1024)S(1)}, u32[]{:S(2)}) copy-start(f32[1240]{0:T(1024)S(1)} %broadcast_multiply_fusion.13) | copy-start | bytes 14884
  587.7 33.5 %slice-start.38 = ((s8[7618560]{0:T(1024)(128)(4,1)}), s8[4194304]{0:T(1024)(128)(4,1)S(1)}, s32[]{:S(2)}) async-start(s8[7618560]{0:T(1024)(128)(4,1)} %bitcast.595), calls=%async_computation.39 | async-start | bytes 8388608
  593.7 26.6 %collective-permute-start.6 = (bf16[1240,512]{1,0:T(8,128)(2,1)S(1)}, bf16[1240,512]{1,0:T(8,128)(2,1)S(1)}, u32[]{:S(2)}, u32[]{:S(2)}) collective-permute-start(bf16[1240,512]{1,0:T(8,128)(2,1)S(1)} %get-tuple-element.179), channel_id=1, source_target_pairs={{0,16},{1,17},{2,18},{3,19},{4,20},{5,21},{6,22},{7,23},{8,24},{9,... | collective-permute-start | bytes 3809288 | tf_op jit(solution)/shard_map/ppermute | solution.py:20
  630.7 28.9 %collective-permute-start.1 = (bf16[1240,512]{1,0:T(8,128)(2,1)S(1)}, bf16[1240,512]{1,0:T(8,128)(2,1)S(1)}, u32[]{:S(2)}, u32[]{:S(2)}) collective-permute-start(bf16[1240,512]{1,0:T(8,128)(2,1)S(1)} %fusion.153), channel_id=1, source_target_pairs={{16,0},{17,1},{18,2},{19,3},{20,4},{21,5},{22,6},{23,7},{24,8},{25... | collective-permute-start | bytes 3809288 | tf_op jit(solution)/shard_map/ppermute | solution.py:20
  805.8 28.3 %collective-permute-start.3 = (bf16[1240,512]{1,0:T(8,128)(2,1)}, bf16[1240,512]{1,0:T(8,128)(2,1)}, u32[]{:S(2)}, u32[]{:S(2)}) collective-permute-start(bf16[1240,512]{1,0:T(8,128)(2,1)} %get-tuple-element.159), channel_id=1, source_target_pairs={{16,0},{17,1},{18,2},{19,3},{20,4},{21,5},{22,6},{23,7},{24,8},{25... | collective-permute-start | bytes 3809288 | tf_op jit(solution)/shard_map/ppermute | solution.py:20
  915.0 48.5 %copy-start.22 = (bf16[1240,1536]{1,0:T(8,128)(2,1)S(1)}, bf16[1240,1536]{1,0:T(8,128)(2,1)}, u32[]{:S(2)}) copy-start(bf16[1240,1536]{1,0:T(8,128)(2,1)} %get-tuple-element.85) | copy-start | bytes 11427844
  1007.8 69.2 %collective-permute-start.5 = (bf16[1240,512]{1,0:T(8,128)(2,1)}, bf16[1240,512]{1,0:T(8,128)(2,1)}, u32[]{:S(2)}, u32[]{:S(2)}) collective-permute-start(bf16[1240,512]{1,0:T(8,128)(2,1)} %get-tuple-element.161), channel_id=1, source_target_pairs={{16,0},{17,1},{18,2},{19,3},{20,4},{21,5},{22,6},{23,7},{24,8},{25... | collective-permute-start | bytes 3809288 | tf_op jit(solution)/shard_map/ppermute | solution.py:20
  1216.2 27.3 %collective-permute-start.7 = (bf16[1240,512]{1,0:T(8,128)(2,1)}, bf16[1240,512]{1,0:T(8,128)(2,1)}, u32[]{:S(2)}, u32[]{:S(2)}) collective-permute-start(bf16[1240,512]{1,0:T(8,128)(2,1)} %get-tuple-element.163), channel_id=1, source_target_pairs={{16,0},{17,1},{18,2},{19,3},{20,4},{21,5},{22,6},{23,7},{24,8},{25... | collective-permute-start | bytes 3809288 | tf_op jit(solution)/shard_map/ppermute | solution.py:20
  1395.4 65.6 %copy-start.204 = (f32[1,512]{1,0:T(1,128)S(1)}, f32[1,512]{1,0:T(1,128)}, u32[]{:S(2)}) copy-start(f32[1,512]{1,0:T(1,128)} %param.22) | copy-start | bytes 6148
  (231 other events, 1717.4 us)
Sparse Core Ops, SparseCore 0:
  1385.7 195.1 all-reduce.13
where the time goes:
time: 1610 us; the launch traced here: 1600 us
  matrix products  545 us (34%)
  local copies, waits for them, and re-layouts  401 us (25%)
  other arithmetic  355 us (22%)
  waiting for transfers between devices  193 us (12%)
  blocking collectives  62.2 us (4%)
  between operations  21.5 us (1%)
  starting transfers between devices  21.2 us (1%)
    dot_general x5, matrix products, layer_forward(): jnp.dot(normed, widen, preferred_element_type=jnp.float32) + hidden_bias  145 us
    reshape x45, local copies, waits for them, and re-layouts, image_blocks(): return rows[first:first + SETS * count].reshape(SETS, count, rows.shape[-1])  118 us
    psum x1, waiting for transfers between devices, shards(): lax.psum((totals[0], totals[1], totals[2], totals[3], totals[4], totals[5...  107 us
    ppermute x8, waiting for transfers between devices, from_behind(): return lax.ppermute(x, axis, pairs)  85.3 us
    dot_general x5, matrix products, layer_backward(): jnp.einsum('rd,cd->rc', grad_branch, narrow, preferred_element_type=jnp.f...  82.1 us
    reduce_sum x3, other arithmetic, layer_backward(): grad_hidden_bias = jnp.sum(grad_hidden, axis=0, dtype=jnp.float32)  79.4 us
    unnamed x515, local copies, waits for them, and re-layouts  66.6 us
    psum x1, blocking collectives, shards(): lax.psum((totals[0], totals[1], totals[2], totals[3], totals[4], totals[5...  62.2 us
  transfers between devices with their start and end apart: 9, of which 6 were waited for; matrix products, arithmetic and copies ran while one was open for 12% of the time, Pallas kernels for 0%

commit v1 on v0

v1 whole, which is shorter than its diff:
```python
import jax
import jax.numpy as jnp
from jax import lax
from jax.experimental import pallas as pl
from jax.experimental.pallas import tpu as pltpu
from jax.sharding import PartitionSpec as P

P_SMALL = 100
P_MID = 196
P_LARGE = 324
EPSILON = 1e-05
BF = jnp.bfloat16
F32 = jnp.float32
MESH = pl.DeviceIdType.MESH
TILE = 256

HALVES = (
    {"first": 0, "rows": 592, "deep": 640, "starts": (0, 192, 384), "win": 208, "wide": 256, "out": 592},
    {"first": 592, "rows": 656, "deep": 768, "starts": (0, 320), "win": 336, "wide": 384, "out": 648},
)
PADDED = 1248
TALL = 768
ONES = 16


def dot(a, b):
    return lax.dot_general(a, b, (((1,), (0,)), ((), ())), preferred_element_type=F32)


def dot_nt(a, b):
    return lax.dot_general(a, b, (((1,), (1,)), ((), ())), preferred_element_type=F32)


def over_rows(rows, step, body):
    def one(index, carry):
        body(pl.multiple_of(index * step, step), step)
        return carry

    lax.fori_loop(0, rows // step, one, 0)
    if rows % step:
        body(rows - rows % step, rows % step)


def over_tiles(count, body):
    def one(index, carry):
        body(pl.multiple_of(index * TILE, TILE))
        return carry

    lax.fori_loop(0, count, one, 0)


def fold8(values):
    rows = values.shape[0]
    total = values[0:8]
    for at in range(8, rows, 8):
        total = total + values[at : at + 8]
    return total


def assemble(parts, starts, rows):
    pieces = []
    win = parts[0].shape[0]
    for index, (part, start) in enumerate(zip(parts, starts)):
        low = 0
        if index > 0:
            low = starts[index - 1] + win - start
            pieces.append(parts[index - 1][win - low :] + part[:low])
        high = win if index == len(parts) - 1 else starts[index + 1] - start
        pieces.append(part[low:high])
    return jnp.concatenate(pieces, axis=0)


def layer_kernel(
    bnd_ref,
    widen_ref,
    narrow_ref,
    sp_a,
    sp_b,
    spt_a,
    spt_b,
    pos_a,
    pos_b,
    eg_ref,
    es_ref,
    hb_ref,
    gg_ref,
    gs_ref,
    ob_ref,
    res_ref,
    wg_ref,
    ng_ref,
    ga_ref,
    gb_ref,
    pa_ref,
    pb_ref,
    gate_ref,
    entry_ref,
    buf,
    n_s,
    nt_s,
    g_s,
    gt_s,
    u_s,
    du_s,
    s_s,
    m_s,
    q_s,
    z_s,
    dv_s,
    wide_s,
    gsp_s,
    gh_s,
    o32,
    stage,
    load_sem,
    send_sem,
    recv_sem,
    out_sem,
):
    section = lax.axis_index("section")
    is_first = section == 0
    partner = {"section": 1 - section}
    micro = bnd_ref.shape[0]
    width = widen_ref.shape[0]
    gate = narrow_ref.shape[0]
    tiles = gate // TILE
    sp = (sp_a, sp_b)
    spt = (spt_a, spt_b)
    pos = (pos_a, pos_b)
    gsp = (ga_ref, gb_ref)
    psum = (pa_ref, pb_ref)

    def load(index, half):
        span = pl.ds(HALVES[half]["first"], HALVES[half]["rows"])
        return pltpu.make_async_copy(
            bnd_ref.at[index, span], buf.at[0, index, span], load_sem.at[index, half]
        )

    def send(index, half):
        span = pl.ds(HALVES[half]["first"], HALVES[half]["rows"])
        return pltpu.make_async_remote_copy(
            src_ref=stage.at[half, pl.ds(0, HALVES[half]["rows"])],
            dst_ref=buf.at[1, index, span],
            send_sem=send_sem.at[index, half],
            recv_sem=recv_sem.at[index, half],
            device_id=partner,
            device_id_type=MESH,
        )

    def store(index, half):
        count = HALVES[half]["out"]
        return pltpu.make_async_copy(
            o32.at[half, pl.ds(0, count)],
            res_ref.at[index, pl.ds(HALVES[half]["first"], count)],
            out_sem.at[half],
        )

    barrier = pltpu.get_barrier_semaphore()
    pl.semaphore_signal(barrier, inc=1, device_id=partner, device_id_type=MESH)

    for index in range(micro):
        for half in range(2):
            load(index, half).start()

    def clear(ref):
        rows = ref.shape[-2]

        def body(at, size):
            ref[pl.ds(at, size), :] = jnp.zeros((size, ref.shape[-1]), ref.dtype)

        over_rows(rows, 16, body)

    for ref in (wg_ref, ng_ref, pa_ref, pb_ref, n_s, g_s, m_s, q_s, gsp_s, gh_s):
        clear(ref)
    for ref in (ga_ref, gb_ref, gate_ref, entry_ref):
        ref[...] = jnp.zeros(ref.shape, ref.dtype)

    pl.semaphore_wait(barrier, 1)

    def forward(step, index, half):
        spec = HALVES[half]
        first, rows = spec["first"], spec["rows"]

        def entry(at, size):
            x = buf[section, index, pl.ds(first + at, size), :].astype(F32)
            centred = x - jnp.mean(x, axis=-1, keepdims=True)
            spread = jnp.mean(centred * centred, axis=-1, keepdims=True)
            normed = centred * lax.rsqrt(spread + EPSILON) * eg_ref[...] + es_ref[...]
            n_s[pl.ds(at, size), :] = normed.astype(BF)

        over_rows(rows, 16, entry)
        if spec["deep"] <= TALL and rows < HALVES[1]["rows"]:
            n_s[rows : spec["deep"], :] = jnp.zeros((spec["deep"] - rows, width), BF)

        def gelu_tile(at):
            hidden = dot(n_s[0:rows, :], widen_ref[:, pl.ds(at, TILE)]) + hb_ref[:, pl.ds(at, TILE)]
            square = hidden * hidden
            curve = jnp.tanh(hidden * (0.7978845608028654 + 0.035677408136300125 * square))
            above = curve + 1.0
            active = (0.5 * hidden) * above
            slope = above * (0.5 + (hidden - active) * (0.7978845608028654 + 0.10703222440890037 * square))
            return active, slope

        def lower(at):
            active, slope = gelu_tile(pl.multiple_of(gate + at, TILE))
            wide_s[0:rows, pl.ds(at, TILE)] = active
            dv_s[0:rows, pl.ds(at, TILE)] = slope.astype(BF)

        over_tiles(tiles, lower)

        def gate_norm(at, size):
            span = pl.ds(at, size)
            v = wide_s[span, :]
            centred = v - jnp.mean(v, axis=-1, keepdims=True)
            spread = jnp.mean(centred * centred, axis=-1, keepdims=True)
            factor = lax.rsqrt(spread + EPSILON)
            z = centred * factor
            z_s[span, :] = z.astype(BF)
            q_s[span, :] = (z * gg_ref[...] + gs_ref[...]).astype(BF)
            dv_s[span, :] = (dv_s[span, :].astype(F32) * factor).astype(BF)

        over_rows(rows, 16, gate_norm)

        def upper(at):
            active, slope = gelu_tile(at)
            u_s[0:rows, pl.ds(at, TILE)] = active.astype(BF)
            du_s[0:rows, pl.ds(at, TILE)] = slope.astype(BF)

        over_tiles(tiles, upper)

        def mix(at):
            parts = [
                dot(sp[half][w], q_s[start : start + spec["wide"], pl.ds(at, TILE)])
                for w, start in enumerate(spec["starts"])
            ]
            mixed = assemble(parts, spec["starts"], rows)
            shift = pos[half][...]
            mixed = mixed + jnp.concatenate([shift, shift], axis=1)
            s_s[0:rows, pl.ds(at, TILE)] = mixed.astype(BF)
            u = u_s[0:rows, pl.ds(at, TILE)].astype(F32)
            m_s[0:rows, pl.ds(at, TILE)] = (u * mixed).astype(BF)

        over_tiles(tiles, mix)

        @pl.when(step < micro)
        def _():
            @pl.when(jnp.logical_and(section == 1, step > 0))
            def _():
                store(index - 1, half).wait()

            @pl.when(jnp.logical_and(is_first, step > 0))
            def _():
                send(index - 1, half).wait_send()

            def project(at):
                x = buf[section, index, first : first + rows, pl.ds(at, TILE)].astype(F32)
                y = dot(m_s[0:rows, :], narrow_ref[:, pl.ds(at, TILE)])
                y = x + (y + ob_ref[:, pl.ds(at, TILE)])

                @pl.when(section == 1)
                def _():
                    o32[half, 0:rows, pl.ds(at, TILE)] = y

                @pl.when(is_first)
                def _():
                    stage[half, 0:rows, pl.ds(at, TILE)] = y.astype(BF)

            over_tiles(width // TILE, project)

            @pl.when(section == 1)
            def _():
                store(index, half).start()

            @pl.when(is_first)
            def _():
                send(index, half).start()

    def backward(step, index, half):
        spec = HALVES[half]
        first, rows, deep = spec["first"], spec["rows"], spec["deep"]
        other = 1 - section

        def cotangent(at, size):
            g = buf[other, index, pl.ds(first + at, size), :]
            g_s[pl.ds(at, size), :] = g
            entry_ref[2] += fold8(g.astype(F32))

        over_rows(rows, 16, cotangent)
        if rows < HALVES[1]["rows"]:
            g_s[rows:deep, :] = jnp.zeros((deep - rows, width), BF)
        gt_s[:, 0:deep] = g_s[0:deep, :].T
        nt_s[0:width, 0:deep] = n_s[0:deep, :].T
        lane = lax.broadcasted_iota(jnp.int32, (ONES, deep), 1)
        nt_s[width : width + ONES, 0:deep] = jnp.where(lane < rows, 1.0, 0.0).astype(BF)

        def narrow_total(at):
            ng_ref[:, pl.ds(at, TILE)] += dot(gt_s[:, 0:deep], m_s[0:deep, pl.ds(at, TILE)])

        over_tiles(tiles, narrow_total)

        def split(at):
            span = pl.ds(at, TILE)
            gm = dot_nt(g_s[0:rows, :], narrow_ref[span, :])
            moved = (gm * u_s[0:rows, span].astype(F32)).astype(BF)
            gsp_s[0:rows, span] = moved
            moved = moved.astype(F32)
            psum[half][...] += moved[:, 0:128] + moved[:, 128:256]
            mixed = s_s[0:rows, span].astype(F32)
            gh_s[0:rows, span] = (gm * mixed * du_s[0:rows, span].astype(F32)).astype(BF)

        over_tiles(tiles, split)

        def unmix(at):
            parts = [
                dot(spt[half][w], gsp_s[start : start + spec["wide"], pl.ds(at, TILE)])
                for w, start in enumerate(spec["starts"])
            ]
            wide_s[0:rows, pl.ds(at, TILE)] = assemble(parts, spec["starts"], rows)

        over_tiles(tiles, unmix)

        for w, start in enumerate(spec["starts"]):
            gsp[half][w] += dot_nt(
                gsp_s[start : start + spec["win"], :], q_s[start : start + spec["wide"], :]
            )

        def gate_back(at, size):
            span = pl.ds(at, size)
            gq = wide_s[span, :]
            z = z_s[span, :].astype(F32)
            gate_ref[0] += fold8(gq * z)
            gate_ref[1] += fold8(gq)
            e = gq * gg_ref[...]
            first_mean = jnp.mean(e, axis=-1, keepdims=True)
            second_mean = jnp.mean(e * z, axis=-1, keepdims=True)
            gv = (e - first_mean - z * second_mean) * dv_s[span, :].astype(F32)
            gh_s[span, gate : 2 * gate] = gv.astype(BF)

        over_rows(rows, 16, gate_back)

        def widen_total(at):
            wg_ref[:, pl.ds(at, TILE)] += dot(nt_s[:, 0:deep], gh_s[0:deep, pl.ds(at, TILE)])

        over_tiles(2 * tiles, widen_total)

        def pull(at):
            wide_s[0:rows, pl.ds(at, TILE)] = dot_nt(
                gh_s[0:rows, :], widen_ref[pl.ds(at, TILE), :]
            )

        over_tiles(width // TILE, pull)

        def entry_back(at, size):
            span = pl.ds(at, size)
            x = buf[section, index, pl.ds(first + at, size), :].astype(F32)
            centred = x - jnp.mean(x, axis=-1, keepdims=True)
            spread = jnp.mean(centred * centred, axis=-1, keepdims=True)
            factor = lax.rsqrt(spread + EPSILON)
            z = centred * factor
            gn = wide_s[span, 0:width]
            entry_ref[0] += fold8(gn * z)
            entry_ref[1] += fold8(gn)
            e = gn * eg_ref[...]
            first_mean = jnp.mean(e, axis=-1, keepdims=True)
            second_mean = jnp.mean(e * z, axis=-1, keepdims=True)
            back = factor * (e - first_mean - z * second_mean)
            gy = buf[other, index, pl.ds(first + at, size), :].astype(F32)
            return span, gy + back

        @pl.when(is_first)
        def _():
            @pl.when(step > micro)
            def _():
                store(index - 1, half).wait()

            def keep(at, size):
                span, gx = entry_back(at, size)
                o32[half, span, :] = gx

            over_rows(rows, 16, keep)
            store(index, half).start()

        @pl.when(section == 1)
        def _():
            @pl.when(step > 0)
            def _():
                send(index - 1, half).wait_send()

            def keep(at, size):
                span, gx = entry_back(at, size)
                stage[half, span, :] = gx.astype(BF)

            over_rows(rows, 16, keep)
            send(index, half).start()

    def one_step(step, carry):
        index = lax.rem(step, micro)
        for half in range(2):

            @pl.when(step < micro)
            def _():
                load(index, half).wait()

            @pl.when(section == 1)
            def _():
                send(index, half).wait_recv()

            forward(step, index, half)

            @pl.when(jnp.logical_and(is_first, step >= micro))
            def _():
                send(index, half).wait_recv()

            @pl.when(jnp.logical_or(section == 1, step >= micro))
            def _():
                backward(step, index, half)

        return carry

    lax.fori_loop(0, micro * (2 - section), one_step, 0)

    for half in range(2):
        store(micro - 1, half).wait()
        send(micro - 1, half).wait_send()


def place(square, offset, rows, columns):
    count = square.shape[0]
    return jnp.pad(square, ((offset, rows - offset - count), (offset, columns - offset - count)))


def windows(squares):
    small, middle, large = squares
    first = place(small, 0, 208, 256) + place(small, P_SMALL, 208, 256)
    return (
        jnp.stack([first, place(middle, 8, 208, 256), place(middle, 12, 208, 256)]),
        jnp.stack([place(large, 0, 336, 384), place(large, 4, 336, 384)]),
    )


def shards(
    boundary,
    entry_gain,
    entry_shift,
    widen_weight,
    hidden_bias,
    gate_gain,
    gate_shift,
    spatial_weight,
    position_bias,
    narrow_weight,
    output_bias,
    crop_starts,
):
    micro, rows_dev, width = boundary.shape[1:]
    hidden = widen_weight.shape[-1]
    gate = hidden // 2
    starts = crop_starts[0]
    spatial = spatial_weight[0]
    position = position_bias[0]
    bnd = jnp.pad(boundary[0], ((0, 0), (0, PADDED - rows_dev), (0, 0)))
    counts = (P_SMALL, P_MID, P_LARGE)
    squares = [
        lax.dynamic_slice(spatial, (starts[k], starts[k]), (c, c)) for k, c in enumerate(counts)
    ]
    shifts = [lax.dynamic_slice(position, (starts[k],), (c,)) for k, c in enumerate(counts)]
    sp_a, sp_b = windows(squares)
    spt_a, spt_b = windows([item.T for item in squares])
    pos_a = jnp.concatenate([shifts[0], shifts[0], shifts[1], shifts[1]])
    pos_b = jnp.pad(jnp.concatenate([shifts[2], shifts[2]]), (0, 8))
    pos_a = jnp.broadcast_to(pos_a[:, None], (592, 128))
    pos_b = jnp.broadcast_to(pos_b[:, None], (656, 128))

    vmem = pl.BlockSpec(memory_space=pltpu.VMEM)
    anywhere = pl.BlockSpec(memory_space=pl.ANY)
    most = HALVES[1]["rows"]
    outs = pl.pallas_call(
        layer_kernel,
        out_shape=(
            jax.ShapeDtypeStruct((micro, rows_dev, width), F32),
            jax.ShapeDtypeStruct((width + ONES, hidden), F32),
            jax.ShapeDtypeStruct((width, gate), F32),
            jax.ShapeDtypeStruct((3, 208, 256), F32),
            jax.ShapeDtypeStruct((2, 336, 384), F32),
            jax.ShapeDtypeStruct((592, 128), F32),
            jax.ShapeDtypeStruct((656, 128), F32),
            jax.ShapeDtypeStruct((2, 8, gate), F32),
            jax.ShapeDtypeStruct((3, 8, width), F32),
        ),
        in_specs=[anywhere] + [vmem] * 14,
        out_specs=[anywhere] + [vmem] * 8,
        scratch_shapes=[
            pltpu.VMEM((2, micro, PADDED, width), BF),
            pltpu.VMEM((TALL, width), BF),
            pltpu.VMEM((width + ONES, TALL), BF),
            pltpu.VMEM((TALL, width), BF),
            pltpu.VMEM((width, TALL), BF),
            pltpu.VMEM((most, gate), BF),
            pltpu.VMEM((most, gate), BF),
            pltpu.VMEM((most, gate), BF),
            pltpu.VMEM((TALL, gate), BF),
            pltpu.VMEM((704, gate), BF),
            pltpu.VMEM((most, gate), BF),
            pltpu.VMEM((most, gate), BF),
            pltpu.VMEM((most, gate), F32),
            pltpu.VMEM((704, gate), BF),
            pltpu.VMEM((TALL, hidden), BF),
            pltpu.VMEM((2, most, width), F32),
            pltpu.VMEM((2, most, width), BF),
            pltpu.SemaphoreType.DMA((micro, 2)),
            pltpu.SemaphoreType.DMA((micro, 2)),
            pltpu.SemaphoreType.DMA((micro, 2)),
            pltpu.SemaphoreType.DMA((2,)),
        ],
        compiler_params=pltpu.CompilerParams(
            collective_id=0, has_side_effects=True, vmem_limit_bytes=63 * 2**20
        ),
        name="layer_relay",
    )(
        bnd,
        widen_weight[0],
        narrow_weight[0],
        sp_a,
        sp_b,
        spt_a,
        spt_b,
        pos_a,
        pos_b,
        entry_gain,
        entry_shift,
        hidden_bias,
        gate_gain,
        gate_shift,
        output_bias,
    )
    results, wide_total, narrow_total, square_a, square_b, line_a, line_b, gate_total, entry_total = outs

    spatial_total = jnp.zeros(spatial.shape, F32)
    position_total = jnp.zeros(position.shape, F32)
    line_a = jnp.sum(line_a, axis=1)
    line_b = jnp.sum(line_b, axis=1)
    square_parts = (
        square_a[0, :100, :100] + square_a[0, 100:200, 100:200],
        square_a[1, 8:204, 8:204] + square_a[2, 12:208, 12:208],
        square_b[0, :324, :324] + square_b[1, 4:328, 4:328],
    )
    line_parts = (
        line_a[0:100] + line_a[100:200],
        line_a[200:396] + line_a[396:592],
        line_b[0:324] + line_b[324:648],
    )
    for k, c in enumerate(counts):
        at = (starts[k], starts[k])
        current = lax.dynamic_slice(spatial_total, at, (c, c))
        spatial_total = lax.dynamic_update_slice(spatial_total, current + square_parts[k], at)
        current = lax.dynamic_slice(position_total, (starts[k],), (c,))
        position_total = lax.dynamic_update_slice(position_total, current + line_parts[k], (starts[k],))
    small = jnp.concatenate(
        [
            jnp.sum(entry_total, axis=1).reshape(-1),
            wide_total[width],
            jnp.sum(gate_total, axis=1).reshape(-1),
            position_total,
        ]
    )
    wide_total, narrow_total, spatial_total, small = lax.psum(
        (wide_total[:width], narrow_total, spatial_total, small), "dp"
    )
    at = 3 * width
    entry_grads = small[:at].reshape(3, width)
    hidden_grads = small[at : at + hidden]
    at = at + hidden
    gate_grads = small[at : at + 2 * gate].reshape(2, gate)
    position_total = small[at + 2 * gate :]
    return (
        results[None],
        entry_grads[None],
        wide_total[None],
        hidden_grads[None],
        gate_grads[None],
        spatial_total[None],
        position_total[None],
        narrow_total.T[None],
    )


def solution(mesh):
    placed = (
        P("section", None, "dp", None),
        P("section", None),
        P("section", None),
        P("section", None, None),
        P("section", None),
        P("section", None),
        P("section", None),
        P("section", None, None),
        P("section", None),
        P("section", None, None),
        P("section", None),
        P("section", None),
    )
    return jax.shard_map(
        shards,
        mesh=mesh,
        in_specs=placed,
        out_specs=(
            P("section", None, "dp", None),
            P("section", None, None),
            P("section", None, None),
            P("section", None),
            P("section", None, None),
            P("section", None, None),
            P("section", None),
            P("section", None, None),
        ),
        check_vma=False,
    )
```

time: 1610 us -> 902 us (0.56)
  Pallas kernels: 0 us -> 639 us
  matrix products: 545 us -> 0 us
  local copies, waits for them, and re-layouts: 401 us -> 48.2 us
  other arithmetic: 355 us -> 4.41 us
  waiting for transfers between devices: 193 us -> 125 us
  starting transfers between devices: 21.2 us -> 0.04 us
    pallas_call x0 -> x1, Pallas kernels: none -> 639 us  [shards(): pl.pallas_call(layer_kernel, out_shape=(jax.ShapeDtypeStruct((micro, rows...]
    dot_general x75 -> x0, matrix products: 545 us -> none  [the longest x5 145 us: layer_forward(): jnp.dot(normed, widen, preferred_element_type=jnp.float32) + hidden_bias]
    reduce_sum x76 -> x4, other arithmetic: 245 us -> 0.41 us  [the longest x1 0.17 us: shards(): line_b = jnp.sum(line_b, axis=1)]
    reshape x75 -> x2, local copies, waits for them, and re-layouts: 221 us -> 0.03 us  [the longest x1 0.02 us: shards(): jnp.sum(gate_total, axis=1).reshape(-1)]
    ppermute x8 -> x0, waiting for transfers between devices: 85.3 us -> none  [from_behind(): return lax.ppermute(x, axis, pairs)]
    slice x46 -> x5, local copies, waits for them, and re-layouts: 60.2 us -> 2.82 us  [the longest x1 1.31 us: shards(): starts[k]]
    unnamed x515 -> x23, local copies, waits for them, and re-layouts: 66.6 us -> 19.1 us
    add_any x5 -> x0, other arithmetic: 35.8 us -> none  [norm_rows(): average = jnp.mean(values, axis=-1, keepdims=True)]
  transfers between devices with their start and end apart: 9 -> 1, of which waited for: 6 -> 1; matrix products, arithmetic and copies ran while one was open for 12% -> 0% of each run, Pallas kernels for 0% -> 0%
where the time goes in v1:
time: 902 us
  Pallas kernels  639 us (71%)
  waiting for transfers between devices  125 us (14%)
  blocking collectives  66.6 us (7%)
  local copies, waits for them, and re-layouts  48.2 us (5%)
  between operations  18.2 us (2%)
    pallas_call x1, Pallas kernels, shards(): pl.pallas_call(layer_kernel, out_shape=(jax.ShapeDtypeStruct((micro, rows...  639 us
    psum x1, waiting for transfers between devices, shards(): lax.psum((wide_total[:width], narrow_total, spatial_total, small), 'dp')  125 us
    psum x1, blocking collectives, shards(): lax.psum((wide_total[:width], narrow_total, spatial_total, small), 'dp')  66.6 us
    unnamed x23, local copies, waits for them, and re-layouts  19.1 us
  transfers between devices with their start and end apart: 1, of which 1 were waited for; matrix products, arithmetic and copies ran while one was open for 0% of the time, Pallas kernels for 0%

profile of v1, /device:TPU:0, one launch (start us, length us, event | category | flops | bytes accessed | tf_op | source)
XLA Modules:
  0.0 901.5 jit_solution(9438727081317373027)
XLA Ops:
  7.2 1.3 fusion.3
  11.1 1.1 copy.22
  12.9 1.0 constant_dynamic-slice_fusion.2
  14.6 0.9 constant_dynamic-slice_fusion.3
  15.5 0.8 constant_dynamic-slice_fusion
  17.5 0.9 copy.23.sp_a
  18.7 1.0 copy.24.sp_b
  20.0 5.2 pad.50.bnd_ref
  25.4 0.8 pad_maximum_fusion.1.spt_b
  26.3 0.8 pad_maximum_fusion.3.spt_a
  27.1 0.8 broadcast_in_dim.36.pos_a
  27.9 0.9 broadcast_in_dim.37.pos_b
  28.8 638.8 %layer_relay.1 = (f32[4,1240,512]{2,1,0:T(8,128)}, f32[528,3072]{1,0:T(8,128)}, f32[512,1536]{1,0:T(8,128)}, f32[3,208,256]{2,1,0:T(8,128)}, f32[2,336,384]{2,1,...) custom-call(bf16[4,1248,512]{2,1,0:T(8,128)(2,1)} %pad.50.bnd_ref, ...), custom_call_target="tpu_custom_call" | custom-call | tf_op jit(solution)/shard_map/layer_relay/pallas_call | solution.py:477
  667.7 6.4 slice_bitcast_fusion
  674.1 1.4 dynamic_update_slice.16
  675.8 3.7 dynamic_update_slice.17
  679.6 1.0 fusion
  680.6 0.9 slice.83
  682.4 66.6 %psum.28 = f32[8004]{0:T(1024)S(1)} all-reduce(f32[8004]{0:T(1024)S(1)} %pad_maximum_fusion.4), channel_id=1, replica_groups=mesh['section'=2,'dp'=16] {'dp'}, use_global_device_ids=true, to_apply=%region_4.5 | all-reduce | flops 8004 | bytes 64032 | tf_op jit(solution)/shard_map/psum | solution.py:566
  751.4 125.2 %all-reduce.17.cloned.1.call-done = (f32[1,512,3072]{2,1,0:T(8,128)}, f32[1,324,324]{2,1,0:T(8,128)}, f32[1,1536,512]{1,2,0:T(8,128)}) async-done(((f32[1,512,3072]{2,1,0:T(8,128)}, f32[1,324,324]{2,1,0:T(8,128)}, f32[1,1536,512]{1,2,0:T(8,128)}), (f32[1,512,3072]{2,1,0:T(8,128)}, f32[1,324,324]{2,1,0:T(8,128)}, f32[1,1536,512]{1,2,0:T(8,128)})) %all-reduce.17.cloned.1.call-update) | async-done | bytes 9857104 | tf_op jit(solution)/shard_map/psum | solution.py:566
  876.7 2.3 copy.25
  879.0 3.7 copy.26
  882.7 9.2 %copy.35 = f32[1,4,1240,512]{3,2,1,0:T(8,128)} copy(f32[1,4,1240,512]{3,2,1,0:T(8,128)} %bitcast.55) | data formatting | bytes 20316160
  892.0 2.7 copy.36
  (53 shorter events, 5.7 us)
Async XLA Ops:
  7.2 12.8 %copy-start.6 = (f32[1,324]{1,0:T(1,128)S(1)}, f32[1,324]{1,0:T(1,128)}, u32[]{:S(2)}) copy-start(f32[1,324]{1,0:T(1,128)} %param.20) | copy-start | bytes 3892
  7.2 869.5 %all-reduce.17.cloned.1.call-start = ((), (), s32[]{:S(2)}) async-start(), calls=%async_computation | async-start | bytes 19881984 | tf_op jit(solution)/shard_map/psum | solution.py:566
  667.6 6.4 copy-start.1
  667.6 11.9 %copy-start = (f32[2,336,384]{2,1,0:T(8,128)S(1)}, f32[2,336,384]{2,1,0:T(8,128)}, u32[]{:S(2)}) copy-start(f32[2,336,384]{2,1,0:T(8,128)} %get-tuple-element.24) | copy-start | bytes 3096580
  675.8 5.7 copy-start.3
  675.8 5.8 copy-start.2
  679.5 2.3 copy-start.4
  679.5 2.4 copy-start.5
  879.0 12.9 %slice-start = ((s8[6291456]{0:T(1024)(128)(4,1)}), s8[2097152]{0:T(1024)(128)(4,1)S(1)}, s32[]{:S(2)}) async-start(s8[6291456]{0:T(1024)(128)(4,1)} %bitcast.56), calls=%async_computation.1 | async-start | bytes 4194304
  882.7 9.3 %slice-start.1 = ((s8[6291456]{0:T(1024)(128)(4,1)}), s8[4194304]{0:T(1024)(128)(4,1)S(1)}, s32[]{:S(2)}) async-start(s8[6291456]{0:T(1024)(128)(4,1)} %bitcast.56), calls=%async_computation.2 | async-start | bytes 8388608
Sparse Core Ops, SparseCore 0:
  680.7 195.9 all-reduce.16

commit v2 on v1

v2 whole, which is shorter than its diff:
```python
import jax
import jax.numpy as jnp
from jax import lax
from jax.experimental import pallas as pl
from jax.experimental.pallas import tpu as pltpu
from jax.sharding import PartitionSpec as P

P_SMALL = 100
P_MID = 196
P_LARGE = 324
EPSILON = 1e-05
BF = jnp.bfloat16
F32 = jnp.float32
MESH = pl.DeviceIdType.MESH
TILE = 256

HALVES = (
    {"first": 0, "rows": 592, "deep": 640, "starts": (0, 192, 384), "win": 208, "wide": 256, "out": 592},
    {"first": 592, "rows": 656, "deep": 768, "starts": (0, 320), "win": 336, "wide": 384, "out": 648},
)
PADDED = 1248
TALL = 768
PART = 32
NARROW_AT = 528
SMALL_AT = 784
SMALL = 112
PACKED = 896
CHUNKS = 7
ONES = 16


def dot(a, b):
    return lax.dot_general(a, b, (((1,), (0,)), ((), ())), preferred_element_type=F32)


def dot_nt(a, b):
    return lax.dot_general(a, b, (((1,), (1,)), ((), ())), preferred_element_type=F32)


def over_rows(rows, step, body, part=None):
    if part is not None:
        inner = body

        def body(at, size):
            for low in range(0, size, part):
                inner(at + low, min(part, size - low))

    def one(index, carry):
        body(pl.multiple_of(index * step, step), step)
        return carry

    if rows // step == 1:
        body(0, step)
    else:
        lax.fori_loop(0, rows // step, one, 0)
    if rows % step:
        body(rows - rows % step, rows % step)


def over_tiles(count, body):
    def one(index, carry):
        body(pl.multiple_of(index * TILE, TILE))
        return carry

    lax.fori_loop(0, count, one, 0)


def fold8(values):
    rows = values.shape[0]
    total = values[0:8]
    for at in range(8, rows, 8):
        total = total + values[at : at + 8]
    return total


def assemble(parts, starts, rows):
    pieces = []
    win = parts[0].shape[0]
    for index, (part, start) in enumerate(zip(parts, starts)):
        low = 0
        if index > 0:
            low = starts[index - 1] + win - start
            pieces.append(parts[index - 1][win - low :] + part[:low])
        high = win if index == len(parts) - 1 else starts[index + 1] - start
        pieces.append(part[low:high])
    return jnp.concatenate(pieces, axis=0)


class Work:
    def __init__(self, names, refs):
        for name, ref in zip(names, refs):
            setattr(self, name, ref)


INPUTS = (
    "bnd", "widen", "narrow", "sp_a", "sp_b", "spt_a", "spt_b", "pos_a", "pos_b",
    "eg", "es", "hb", "gg", "gs", "ob",
)
OUTPUTS = ("res", "packed")
SCRATCH = (
    "wg", "ng", "ga", "gb", "pa", "pb", "gate_sum", "entry_sum",
    "buf", "n", "nt", "g", "gt", "u", "s", "m", "q", "z", "wide", "gh",
    "stage", "kept", "load_sem", "send_sem", "recv_sem", "out_sem",
    "ready", "across_send", "across_recv", "around_send", "around_recv", "own_sem",
)


def row_stats(x):
    centred = x - jnp.mean(x, axis=-1, keepdims=True)
    spread = jnp.mean(centred * centred, axis=-1, keepdims=True)
    return centred, lax.rsqrt(spread + EPSILON)


def entry_norm(w, half, x_at):
    spec = HALVES[half]

    def body(at, size):
        centred, factor = row_stats(x_at(at, size).astype(F32))
        w.n[pl.ds(at, size), :] = (centred * factor * w.eg[...] + w.es[...]).astype(BF)

    over_rows(spec["rows"], 336, body, PART)
    if spec["rows"] < HALVES[1]["rows"]:
        w.n[spec["rows"] : spec["deep"], :] = jnp.zeros((spec["deep"] - spec["rows"], w.n.shape[1]), BF)


def gelu_tile(w, rows, at):
    hidden = dot(w.n[0:rows, :], w.widen[:, pl.ds(at, TILE)]) + w.hb[:, pl.ds(at, TILE)]
    square = hidden * hidden
    curve = jnp.tanh(hidden * (0.7978845608028654 + 0.035677408136300125 * square))
    above = curve + 1.0
    active = (0.5 * hidden) * above
    slope = above * (0.5 + (hidden - active) * (0.7978845608028654 + 0.10703222440890037 * square))
    return active, slope


def lower_half(w, half):
    rows, gate = HALVES[half]["rows"], w.narrow.shape[0]

    def body(at):
        active, slope = gelu_tile(w, rows, pl.multiple_of(gate + at, TILE))
        w.wide[0:rows, pl.ds(at, TILE)] = active
        w.gh[0:rows, pl.ds(pl.multiple_of(gate + at, TILE), TILE)] = slope.astype(BF)

    over_tiles(gate // TILE, body)


def gate_norm(w, half):
    gate = w.narrow.shape[0]

    def body(at, size):
        span = pl.ds(at, size)
        centred, factor = row_stats(w.wide[span, :])
        z = centred * factor
        w.z[span, :] = z.astype(BF)
        w.q[span, :] = (z * w.gg[...] + w.gs[...]).astype(BF)
        w.gh[span, gate:] = (w.gh[span, gate:].astype(F32) * factor).astype(BF)

    over_rows(HALVES[half]["rows"], 336, body, PART)


def upper_half(w, half):
    rows, gate = HALVES[half]["rows"], w.narrow.shape[0]

    def body(at):
        active, slope = gelu_tile(w, rows, at)
        w.u[0:rows, pl.ds(at, TILE)] = active.astype(BF)
        w.gh[0:rows, pl.ds(at, TILE)] = slope.astype(BF)

    over_tiles(gate // TILE, body)


def mix(w, half):
    spec, gate = HALVES[half], w.narrow.shape[0]
    rows = spec["rows"]
    square, shift = (w.sp_a, w.sp_b)[half], (w.pos_a, w.pos_b)[half]

    def body(at):
        span = pl.ds(at, TILE)
        parts = [
            dot(square[i], w.q[start : start + spec["wide"], span])
            for i, start in enumerate(spec["starts"])
        ]
        line = shift[...]
        mixed = assemble(parts, spec["starts"], rows) + jnp.concatenate([line, line], axis=1)
        w.s[0:rows, span] = mixed.astype(BF)
        w.m[0:rows, span] = (w.u[0:rows, span].astype(F32) * mixed).astype(BF)

    over_tiles(gate // TILE, body)


def project(w, half, x_at, keep):
    rows = HALVES[half]["rows"]

    def body(at):
        span = pl.ds(at, TILE)
        y = dot(w.m[0:rows, :], w.narrow[:, span])
        keep(span, x_at(0, rows, span).astype(F32) + (y + w.ob[:, span]))

    over_tiles(w.narrow.shape[1] // TILE, body)


def cotangent(w, half, gy_at):
    spec = HALVES[half]
    rows, deep, width = spec["rows"], spec["deep"], w.narrow.shape[1]

    def body(at, size):
        g = gy_at(at, size)
        w.g[pl.ds(at, size), :] = g
        w.entry_sum[2] += fold8(g.astype(F32))

    over_rows(rows, rows, body)
    if rows < HALVES[1]["rows"]:
        w.g[rows:deep, :] = jnp.zeros((deep - rows, width), BF)
    w.gt[:, 0:deep] = w.g[0:deep, :].T
    w.nt[0:width, 0:deep] = w.n[0:deep, :].T
    lane = lax.broadcasted_iota(jnp.int32, (ONES, deep), 1)
    w.nt[width : width + ONES, 0:deep] = jnp.where(lane < rows, 1.0, 0.0).astype(BF)


def narrow_total(w, half):
    deep = HALVES[half]["deep"]

    def body(at):
        span = pl.ds(at, TILE)
        w.ng[:, span] += dot(w.gt[:, 0:deep], w.m[0:deep, span])

    over_tiles(w.narrow.shape[0] // TILE, body)


def split(w, half):
    rows = HALVES[half]["rows"]
    line = (w.pa, w.pb)[half]

    def body(at):
        span = pl.ds(at, TILE)
        gm = dot_nt(w.g[0:rows, :], w.narrow[span, :])
        moved = (gm * w.u[0:rows, span].astype(F32)).astype(BF)
        mixed = w.s[0:rows, span].astype(F32)
        w.s[0:rows, span] = moved
        moved = moved.astype(F32)
        line[...] += moved[:, 0:128] + moved[:, 128:256]
        w.gh[0:rows, span] = (gm * mixed * w.gh[0:rows, span].astype(F32)).astype(BF)

    over_tiles(w.narrow.shape[0] // TILE, body)


def unmix(w, half):
    spec = HALVES[half]
    square = (w.spt_a, w.spt_b)[half]

    def body(at):
        span = pl.ds(at, TILE)
        parts = [
            dot(square[i], w.s[start : start + spec["wide"], span])
            for i, start in enumerate(spec["starts"])
        ]
        w.wide[0 : spec["rows"], span] = assemble(parts, spec["starts"], spec["rows"])

    over_tiles(w.narrow.shape[0] // TILE, body)


def spatial_total(w, half):
    spec = HALVES[half]
    total = (w.ga, w.gb)[half]
    for i, start in enumerate(spec["starts"]):
        total[i] += dot_nt(w.s[start : start + spec["win"], :], w.q[start : start + spec["wide"], :])


def gate_back(w, half):
    gate = w.narrow.shape[0]

    def body(at, size):
        span = pl.ds(at, size)
        gq = w.wide[span, :]
        z = w.z[span, :].astype(F32)
        w.gate_sum[0] += fold8(gq * z)
        w.gate_sum[1] += fold8(gq)
        e = gq * w.gg[...]
        first_mean = jnp.mean(e, axis=-1, keepdims=True)
        second_mean = jnp.mean(e * z, axis=-1, keepdims=True)
        gv = (e - first_mean - z * second_mean) * w.gh[span, gate:].astype(F32)
        w.gh[span, gate : 2 * gate] = gv.astype(BF)

    over_rows(HALVES[half]["rows"], 336, body, PART)


def widen_total(w, half):
    deep = HALVES[half]["deep"]

    def body(at):
        span = pl.ds(at, TILE)
        w.wg[:, span] += dot(w.nt[:, 0:deep], w.gh[0:deep, span])

    over_tiles(w.widen.shape[1] // TILE, body)


def pull(w, half):
    rows = HALVES[half]["rows"]

    def body(at):
        w.wide[0:rows, pl.ds(at, TILE)] = dot_nt(w.gh[0:rows, :], w.widen[pl.ds(at, TILE), :])

    over_tiles(w.widen.shape[0] // TILE, body)


def entry_back(w, half, x_at, gy_at, keep):
    width = w.widen.shape[0]

    def body(at, size):
        span = pl.ds(at, size)
        centred, factor = row_stats(x_at(at, size).astype(F32))
        z = centred * factor
        gn = w.wide[span, 0:width]
        w.entry_sum[0] += fold8(gn * z)
        w.entry_sum[1] += fold8(gn)
        e = gn * w.eg[...]
        first_mean = jnp.mean(e, axis=-1, keepdims=True)
        second_mean = jnp.mean(e * z, axis=-1, keepdims=True)
        keep(span, gy_at(at, size).astype(F32) + factor * (e - first_mean - z * second_mean))

    over_rows(HALVES[half]["rows"], 336, body, PART)


def clear(ref):
    def body(at, size):
        ref[pl.ds(at, size), :] = jnp.zeros((size, ref.shape[-1]), ref.dtype)

    over_rows(ref.shape[-2], 32, body)


def clear_all(w):
    for ref in (w.wg, w.ng, w.pa, w.pb, w.n, w.g, w.m, w.q, w.s, w.gh):
        clear(ref)
    for ref in (w.ga, w.gb, w.gate_sum, w.entry_sum):
        ref[...] = jnp.zeros(ref.shape, ref.dtype)


class Group:
    def __init__(self):
        at = lax.axis_index("dp")
        self.core = lax.rem(at, 2)
        self.x = lax.rem(at // 2, 2)
        self.z = at // 4
        self.beside = {"dp": at + 1 - 2 * self.core}
        self.across = {"dp": at + 2 - 4 * self.x}
        self.far = [lax.rem(self.z + off, 4) for off in (1, 2, 3)]
        self.around = [{"dp": far * 4 + lax.rem(at, 4)} for far in self.far]
        self.everyone = [self.beside, self.across] + self.around


def turn(values, rows, lanes):
    if rows:
        values = pltpu.roll(values, values.shape[0] - rows, 0)
    if lanes:
        values = pltpu.roll(values, values.shape[1] - lanes, 1)
    return values


def pack(w):
    gate, width = w.narrow.shape
    w.wg[width + 1 : width + 2, 0:gate] = jnp.sum(w.gate_sum[0], axis=0, keepdims=True)
    w.wg[width + 1 : width + 2, gate:] = jnp.sum(w.gate_sum[1], axis=0, keepdims=True)
    for k in range(3):
        w.wg[width + 2 : width + 3, k * width : (k + 1) * width] = jnp.sum(
            w.entry_sum[k], axis=0, keepdims=True
        )
    clear(w.gh.at[SMALL_AT:PACKED])

    def body(at, size):
        w.gh[pl.ds(at, size), :] = w.wg[pl.ds(at, size), :].astype(BF)

    over_rows(w.wg.shape[0], 48, body)
    for b in range(6):
        w.gh[NARROW_AT:SMALL_AT, b * 512 : (b + 1) * 512] = w.ng[:, b * 256 : (b + 1) * 256].T.astype(BF)

    def put(block, lane, first):
        for b in range(0, block.shape[0], SMALL):
            rows = block[b : b + SMALL]
            at = (first + b // SMALL) * 512 + lane
            w.gh[SMALL_AT : SMALL_AT + rows.shape[0], at : at + rows.shape[1]] = rows.astype(BF)

    def with_line(block, line):
        sums = jnp.sum(line[0 : block.shape[0]], axis=1, keepdims=True)
        last = lax.broadcasted_iota(jnp.int32, block.shape, 1) == block.shape[1] - 1
        return jnp.where(last, sums, block)

    line_a, line_b = w.pa[...], w.pb[...]
    large = w.gb[0] + turn(w.gb[1], 4, 4)
    put(with_line(large, line_b + turn(line_b, 324, 0)), 0, 0)
    small = (w.ga[0] + turn(w.ga[0], P_SMALL, P_SMALL))[:, 0:128]
    put(with_line(small, line_a + turn(line_a, P_SMALL, 0)), 384, 0)
    middle = turn(w.ga[1], 8, 8) + turn(w.ga[2], 12, 12)
    put(with_line(middle, turn(line_a, 200, 0) + turn(line_a, 396, 0)), 0, 3)


def add_up(w, group):
    part = PACKED // 4 // CHUNKS
    wide = w.gh.shape[1]
    sides = ((w.m, 0), (w.q, wide // 2))
    quarter = wide // 4

    def rows_at(core, chunk, x):
        return pl.multiple_of(core * (PACKED // 2) + (2 * chunk + x) * part, 16)

    def remote(src, dst, send, recv, to):
        return pltpu.make_async_remote_copy(
            src_ref=src, dst_ref=dst, send_sem=send, recv_sem=recv, device_id=to, device_id_type=MESH
        )

    def halves(chunk, side):
        land, column = sides[side]
        return remote(
            w.gh.at[pl.ds(rows_at(1 - group.core, chunk, 0), 2 * part), pl.ds(column, wide // 2)],
            land.at[pl.ds(2 * chunk * part, 2 * part)],
            w.across_send.at[side, chunk],
            w.across_recv.at[side, chunk],
            group.beside,
        )

    def quarters(chunk, side):
        land, column = sides[side]
        return remote(
            w.gh.at[pl.ds(rows_at(group.core, chunk, 1 - group.x), part), pl.ds(column, wide // 2)],
            land.at[pl.ds(PACKED // 2 + chunk * part, part)],
            w.across_send.at[2 + side, chunk],
            w.across_recv.at[2 + side, chunk],
            group.across,
        )

    def column_of(z):
        return pl.ds(pl.multiple_of(z * quarter, 128), quarter)

    def landed(chunk, k):
        row = (k // 2) * (PACKED // 4) + chunk * part
        return w.z.at[pl.ds(row, part), pl.ds((k % 2) * quarter, quarter)]

    def shares(chunk, k):
        return remote(
            w.gh.at[pl.ds(rows_at(group.core, chunk, group.x), part), column_of(group.far[k])],
            landed(chunk, k),
            w.around_send.at[0, k, chunk],
            w.around_recv.at[0, k, chunk],
            group.around[k],
        )

    def total_of(chunk):
        return w.u.at[pl.ds(chunk * part, part), pl.ds(0, quarter)]

    def own_place(chunk):
        return w.packed.at[pl.ds(rows_at(group.core, chunk, group.x), part), column_of(group.z)]

    def back_around(chunk, k):
        return remote(
            total_of(chunk),
            own_place(chunk),
            w.around_send.at[1, k, chunk],
            w.around_recv.at[1, k, chunk],
            group.around[k],
        )

    def own(chunk):
        return pltpu.make_async_copy(total_of(chunk), own_place(chunk), w.own_sem.at[chunk])

    def back_across(chunk):
        span = pl.ds(rows_at(group.core, chunk, group.x), part)
        return remote(
            w.packed.at[span],
            w.packed.at[span],
            w.across_send.at[4, chunk],
            w.across_recv.at[4, chunk],
            group.across,
        )

    def back_beside(chunk):
        span = pl.ds(rows_at(group.core, chunk, 0), 2 * part)
        return remote(
            w.packed.at[span],
            w.packed.at[span],
            w.across_send.at[5, chunk],
            w.across_recv.at[5, chunk],
            group.beside,
        )

    def accumulate(at, side, row, size):
        land, column = sides[side]
        rows, columns = pl.ds(at, size), pl.ds(column, wide // 2)
        total = w.gh[rows, columns].astype(F32) + land[row : row + size, :].astype(F32)
        w.gh[rows, columns] = total.astype(BF)

    for chunk in range(CHUNKS):
        for side in range(2):
            halves(chunk, side).start()
    for chunk in range(CHUNKS):
        for side in range(2):
            halves(chunk, side).wait_recv()
            accumulate(rows_at(group.core, chunk, 0), side, 2 * chunk * part, 2 * part)
            quarters(chunk, side).start()
    for chunk in range(CHUNKS):
        for side in range(2):
            quarters(chunk, side).wait_recv()
            accumulate(rows_at(group.core, chunk, group.x), side, PACKED // 2 + chunk * part, part)
        for k in range(3):
            shares(chunk, k).start()
    for chunk in range(CHUNKS):
        total = w.gh[pl.ds(rows_at(group.core, chunk, group.x), part), column_of(group.z)].astype(F32)
        for k in range(3):
            shares(chunk, k).wait_recv()
            total = total + landed(chunk, k)[...].astype(F32)
        total_of(chunk)[...] = total.astype(BF)
        own(chunk).start()
        for k in range(3):
            back_around(chunk, k).start()
    for chunk in range(CHUNKS):
        own(chunk).wait()
        for k in range(3):
            back_around(chunk, k).wait_recv()
        back_across(chunk).start()
    for chunk in range(CHUNKS):
        back_across(chunk).wait_recv()
        back_beside(chunk).start()
    for chunk in range(CHUNKS):
        back_beside(chunk).wait_recv()
    for chunk in range(CHUNKS):
        for side in range(2):
            halves(chunk, side).wait_send()
            quarters(chunk, side).wait_send()
        back_across(chunk).wait_send()
        back_beside(chunk).wait_send()
        for k in range(3):
            shares(chunk, k).wait_send()
            back_around(chunk, k).wait_send()


def layer_kernel(*refs):
    w = Work(INPUTS + OUTPUTS + SCRATCH, refs)
    section = lax.axis_index("section")
    is_first = section == 0
    is_second = section == 1
    partner = {"section": 1 - section}
    micro = w.bnd.shape[0]

    def place_of(slot, index, half):
        row = (slot * micro + index) * PADDED + HALVES[half]["first"]
        return pl.ds(pl.multiple_of(row, 16), HALVES[half]["rows"])

    def load(index, half):
        span = pl.ds(HALVES[half]["first"], HALVES[half]["rows"])
        return pltpu.make_async_copy(
            w.bnd.at[index, span], w.buf.at[place_of(0, index, half)], w.load_sem.at[index, half]
        )

    def send(index, half):
        return pltpu.make_async_remote_copy(
            src_ref=w.stage.at[half, pl.ds(0, HALVES[half]["rows"])],
            dst_ref=w.buf.at[place_of(1, index, half)],
            send_sem=w.send_sem.at[index, half],
            recv_sem=w.recv_sem.at[index, half],
            device_id=partner,
            device_id_type=MESH,
        )

    def store(index, half):
        count = HALVES[half]["rows"]
        return pltpu.make_async_copy(
            w.kept.at[half, pl.ds(0, count)],
            w.res.at[index, pl.ds(HALVES[half]["first"], count)],
            w.out_sem.at[half],
        )

    barrier = pltpu.get_barrier_semaphore()
    group = Group() if lax.axis_size("dp") == 16 else None
    others = [partner] if group is None else [partner] + group.everyone
    for other in others:
        pl.semaphore_signal(barrier, inc=1, device_id=other, device_id_type=MESH)
    for index in range(micro):
        for half in range(2):
            load(index, half).start()
    clear_all(w)
    pl.semaphore_wait(barrier, len(others))

    def rows_of(slot, index, half):
        row = (slot * micro + index) * PADDED + HALVES[half]["first"]

        def read(at, size, columns=slice(None)):
            return w.buf[pl.ds(pl.multiple_of(row + at, 16), size), columns]

        return read

    def forward(step, index, half):
        rows = HALVES[half]["rows"]
        x_at = rows_of(section, index, half)
        entry_norm(w, half, x_at)
        lower_half(w, half)
        gate_norm(w, half)
        upper_half(w, half)
        mix(w, half)

        @pl.when(step < micro)
        def _():
            @pl.when(jnp.logical_and(is_second, step > 0))
            def _():
                store(index - 1, half).wait()

            @pl.when(jnp.logical_and(is_first, step > 0))
            def _():
                send(index - 1, half).wait_send()

            def keep(span, y):
                @pl.when(is_second)
                def _():
                    w.kept[half, 0:rows, span] = y.astype(BF)

                @pl.when(is_first)
                def _():
                    w.stage[half, 0:rows, span] = y.astype(BF)

            project(w, half, x_at, keep)

            @pl.when(is_second)
            def _():
                store(index, half).start()

            @pl.when(is_first)
            def _():
                send(index, half).start()

    def backward(step, index, half):
        x_at = rows_of(section, index, half)
        gy_at = rows_of(1 - section, index, half)
        cotangent(w, half, gy_at)
        narrow_total(w, half)
        split(w, half)
        unmix(w, half)
        spatial_total(w, half)
        gate_back(w, half)
        widen_total(w, half)
        pull(w, half)

        @pl.when(is_first)
        def _():
            @pl.when(step > micro)
            def _():
                store(index - 1, half).wait()

            def keep(span, gx):
                w.kept[half, span, :] = gx.astype(BF)

            entry_back(w, half, x_at, gy_at, keep)
            store(index, half).start()

        @pl.when(is_second)
        def _():
            @pl.when(step > 0)
            def _():
                send(index - 1, half).wait_send()

            def keep(span, gx):
                w.stage[half, span, :] = gx.astype(BF)

            entry_back(w, half, x_at, gy_at, keep)
            send(index, half).start()

    def one_step(step, carry):
        index = lax.rem(step, micro)
        for half in range(2):

            @pl.when(step < micro)
            def _():
                load(index, half).wait()

            @pl.when(is_second)
            def _():
                send(index, half).wait_recv()

            forward(step, index, half)

            @pl.when(jnp.logical_and(is_first, step >= micro))
            def _():
                send(index, half).wait_recv()

            @pl.when(jnp.logical_or(is_second, step >= micro))
            def _():
                backward(step, index, half)

        return carry

    lax.fori_loop(0, micro * (2 - section), one_step, 0)

    for half in range(2):
        store(micro - 1, half).wait()
        send(micro - 1, half).wait_send()

    if group is not None:
        for other in group.everyone:
            pl.semaphore_signal(w.ready, inc=1, device_id=other, device_id_type=MESH)
    pack(w)
    if group is None:
        whole = pltpu.make_async_copy(w.gh, w.packed, w.own_sem.at[0])
        whole.start()
        whole.wait()
    else:
        pl.semaphore_wait(w.ready, len(group.everyone))
        add_up(w, group)


def scratch_of(micro, width, hidden):
    gate, most = hidden // 2, HALVES[1]["rows"]
    return [
        pltpu.VMEM((width + ONES, hidden), F32),
        pltpu.VMEM((width, gate), F32),
        pltpu.VMEM((3, 208, 256), F32),
        pltpu.VMEM((2, 336, 384), F32),
        pltpu.VMEM((592, 128), F32),
        pltpu.VMEM((656, 128), F32),
        pltpu.VMEM((2, 8, gate), F32),
        pltpu.VMEM((3, 8, width), F32),
        pltpu.VMEM((2 * micro * PADDED, width), BF),
        pltpu.VMEM((TALL, width), BF),
        pltpu.VMEM((width + ONES, TALL), BF),
        pltpu.VMEM((TALL, width), BF),
        pltpu.VMEM((width, TALL), BF),
        pltpu.VMEM((most, gate), BF),
        pltpu.VMEM((704, gate), BF),
        pltpu.VMEM((TALL, gate), BF),
        pltpu.VMEM((704, gate), BF),
        pltpu.VMEM((most, gate), BF),
        pltpu.VMEM((most, gate), F32),
        pltpu.VMEM((PACKED, hidden), BF),
        pltpu.VMEM((2, most, width), BF),
        pltpu.VMEM((2, most, width), BF),
        pltpu.SemaphoreType.DMA((micro, 2)),
        pltpu.SemaphoreType.DMA((micro, 2)),
        pltpu.SemaphoreType.DMA((micro, 2)),
        pltpu.SemaphoreType.DMA((2,)),
        pltpu.SemaphoreType.REGULAR,
        pltpu.SemaphoreType.DMA((6, CHUNKS)),
        pltpu.SemaphoreType.DMA((6, CHUNKS)),
        pltpu.SemaphoreType.DMA((2, 3, CHUNKS)),
        pltpu.SemaphoreType.DMA((2, 3, CHUNKS)),
        pltpu.SemaphoreType.DMA((CHUNKS,)),
    ]


def outputs_of(micro, width, hidden):
    return (
        jax.ShapeDtypeStruct((micro, PADDED, width), BF),
        jax.ShapeDtypeStruct((PACKED, hidden), BF),
    )


def place(square, offset, rows, columns):
    count = square.shape[0]
    return jnp.pad(square, ((offset, rows - offset - count), (offset, columns - offset - count)))


def windows(squares):
    small, middle, large = squares
    first = place(small, 0, 208, 256) + place(small, P_SMALL, 208, 256)
    return (
        jnp.stack([first, place(middle, 8, 208, 256), place(middle, 12, 208, 256)]),
        jnp.stack([place(large, 0, 336, 384), place(large, 4, 336, 384)]),
    )


def shards(
    boundary,
    entry_gain,
    entry_shift,
    widen_weight,
    hidden_bias,
    gate_gain,
    gate_shift,
    spatial_weight,
    position_bias,
    narrow_weight,
    output_bias,
    crop_starts,
):
    micro, rows_dev, width = boundary.shape[1:]
    hidden = widen_weight.shape[-1]
    gate = hidden // 2
    starts = crop_starts[0]
    spatial = spatial_weight[0]
    position = position_bias[0]
    bnd = jnp.pad(boundary[0], ((0, 0), (0, PADDED - rows_dev), (0, 0)))
    counts = (P_SMALL, P_MID, P_LARGE)
    squares = [
        lax.dynamic_slice(spatial, (starts[k], starts[k]), (c, c)) for k, c in enumerate(counts)
    ]
    shifts = [lax.dynamic_slice(position, (starts[k],), (c,)) for k, c in enumerate(counts)]
    sp_a, sp_b = windows(squares)
    spt_a, spt_b = windows([item.T for item in squares])
    pos_a = jnp.concatenate([shifts[0], shifts[0], shifts[1], shifts[1]])
    pos_b = jnp.pad(jnp.concatenate([shifts[2], shifts[2]]), (0, 8))
    pos_a = jnp.broadcast_to(pos_a[:, None], (592, 128))
    pos_b = jnp.broadcast_to(pos_b[:, None], (656, 128))

    vmem = pl.BlockSpec(memory_space=pltpu.VMEM)
    anywhere = pl.BlockSpec(memory_space=pl.ANY)
    outs = pl.pallas_call(
        layer_kernel,
        out_shape=outputs_of(micro, width, hidden),
        in_specs=[anywhere] + [vmem] * 14,
        out_specs=[anywhere] * 2,
        scratch_shapes=scratch_of(micro, width, hidden),
        compiler_params=pltpu.CompilerParams(
            collective_id=0, has_side_effects=True, vmem_limit_bytes=int(63.9 * 2**20)
        ),
        name="layer_relay",
    )(
        bnd,
        widen_weight[0],
        narrow_weight[0],
        sp_a,
        sp_b,
        spt_a,
        spt_b,
        pos_a,
        pos_b,
        entry_gain,
        entry_shift,
        hidden_bias,
        gate_gain,
        gate_shift,
        output_bias,
    )
    results, packed = outs
    if lax.axis_size("dp") != 16:
        packed = lax.psum(packed.astype(F32), "dp").astype(BF)
    widen_grad = packed[:width].astype(F32)
    narrow_grad = jnp.concatenate(
        [packed[NARROW_AT:SMALL_AT, at : at + width] for at in range(0, hidden, width)]
    ).astype(F32)
    lines = packed[width : width + 3].astype(F32)
    hidden_grads = lines[0]
    gate_grads = lines[1].reshape(2, gate)
    entry_grads = lines[2, : 3 * width].reshape(3, width)
    strips = [packed[SMALL_AT:, at : at + width] for at in range(0, 5 * width, width)]
    upper, lower = jnp.concatenate(strips[:3]).astype(F32), jnp.concatenate(strips[3:]).astype(F32)

    def spread(block, count, start):
        most = P_LARGE - count
        padded = jnp.pad(block, [(most, most)] * block.ndim)
        return lax.dynamic_slice(padded, (most - start,) * block.ndim, (P_LARGE,) * block.ndim)

    spatial_total = (
        upper[:P_LARGE, :P_LARGE]
        + spread(upper[:P_SMALL, 384 : 384 + P_SMALL], P_SMALL, starts[0])
        + spread(lower[:P_MID, :P_MID], P_MID, starts[1])
    )
    position_total = (
        upper[:P_LARGE, 383]
        + spread(upper[:P_SMALL, 511], P_SMALL, starts[0])
        + spread(lower[:P_MID, 255], P_MID, starts[1])
    )
    return (
        results[None, :, :rows_dev].astype(F32),
        entry_grads[None],
        widen_grad[None],
        hidden_grads[None],
        gate_grads[None],
        spatial_total[None],
        position_total[None],
        narrow_grad[None],
    )


def solution(mesh):
    placed = (
        P("section", None, "dp", None),
        P("section", None),
        P("section", None),
        P("section", None, None),
        P("section", None),
        P("section", None),
        P("section", None),
        P("section", None, None),
        P("section", None),
        P("section", None, None),
        P("section", None),
        P("section", None),
    )
    return jax.shard_map(
        shards,
        mesh=mesh,
        in_specs=placed,
        out_specs=(
            P("section", None, "dp", None),
            P("section", None, None),
            P("section", None, None),
            P("section", None),
            P("section", None, None),
            P("section", None, None),
            P("section", None),
            P("section", None, None),
        ),
        check_vma=False,
    )
```

time: 902 us -> 460 us (0.51)
  Pallas kernels: 639 us -> 415 us
  waiting for transfers between devices: 125 us -> 0 us
  blocking collectives: 66.6 us -> 0 us
  local copies, waits for them, and re-layouts: 48.2 us -> 20.5 us
  other arithmetic: 4.41 us -> 16.4 us
  between operations: 18.2 us -> 7.26 us
    pallas_call x1, Pallas kernels: 639 us -> 415 us  [shards(): pl.pallas_call(layer_kernel, out_shape=outputs_of(micro, width, hidden),...]
    psum x1 -> x0, waiting for transfers between devices: 125 us -> none  [shards(): lax.psum((wide_total[:width], narrow_total, spatial_total, small), 'dp')]
    psum x1 -> x0, blocking collectives: 66.6 us -> none  [shards(): lax.psum((wide_total[:width], narrow_total, spatial_total, small), 'dp')]
    unnamed x23 -> x13, local copies, waits for them, and re-layouts: 19.1 us -> 2.54 us
  transfers between devices with their start and end apart: 1 -> 0, of which waited for: 1 -> 0; matrix products, arithmetic and copies ran while one was open for 0% -> 0% of each run, Pallas kernels for 0% -> 0%
where the time goes in v2:
time: 460 us; the launch traced here: 459 us
  Pallas kernels  415 us (90%)
  local copies, waits for them, and re-layouts  20.5 us (4%)
  other arithmetic  16.4 us (4%)
  between operations  7.26 us (2%)
    pallas_call x1, Pallas kernels, shards(): pl.pallas_call(layer_kernel, out_shape=outputs_of(micro, width, hidden),...  415 us

profile of v2, /device:TPU:0, one launch (start us, length us, event | category | flops | bytes accessed | tf_op | source)
XLA Modules:
  0.0 459.2 jit_solution(10070774023479495517)
XLA Ops:
  0.6 1.3 fusion.7
  8.4 0.8 fusion.5
  9.2 0.8 constant_dynamic-slice_fusion
  9.9 0.7 reduce
  10.8 0.9 constant_dynamic-slice_fusion.3
  11.8 1.0 constant_dynamic-slice_fusion.2
  13.0 1.1 copy.29
  14.1 0.9 broadcast_in_dim.26.refs_7_
  15.1 0.8 pad_maximum_fusion.3.refs_5_
  15.9 0.9 broadcast_in_dim.27.refs_8_
  17.0 0.9 copy.30.refs_3_
  18.1 0.8 pad_maximum_fusion.1.refs_6_
  19.2 1.0 copy.31.refs_4_
  20.2 5.2 %pad.66.refs_0_ = bf16[4,1248,512]{2,1,0:T(8,128)(2,1)} pad(bf16[4,1240,512]{2,1,0:T(8,128)(2,1)} %bitcast.58, bf16[]{:T(256)} %constant.14.clone.1), padding=0_0x0_8x0_0 | pad | bytes 10190850 | tf_op jit(solution)/shard_map/jit(_pad)/pad | solution.py:785
  25.5 415.1 %layer_relay.1 = (bf16[4,1248,512]{2,1,0:T(8,128)(2,1)}, bf16[896,3072]{1,0:T(8,128)(2,1)}) custom-call(bf16[4,1248,512]{2,1,0:T(8,128)(2,1)} %pad.66.refs_0_, bf16[512,3072]{1,0:T(8,128)(2,1)} %bitcast.61, bf16[1536,512]{1,0:T(8,128)(2,1)} %bitcast.64, bf16[3,208,256]{2,1,0:T(8,128)(2,1)} %copy.30.refs_3_, bf16[2,336,384]{2,1,0:T(8,128)(2,1)} %copy.31.refs_4_, ...), custom_call_target="tpu_custom_call" | custom-call | tf_op jit(solution)/shard_map/layer_relay/pallas_call | solution.py:800
  440.6 0.8 slice_convert_fusion
  442.0 0.6 slice_reduce_fusion
  442.6 0.6 broadcast_in_dim_reshape_squeeze.7
  443.2 1.3 fusion.6
  445.9 0.7 fusion.1
  446.5 1.3 copy.33
  448.0 3.7 bitcast_convert_fusion.1
  451.7 2.1 convert_element_type.61
  453.8 5.4 %bitcast_convert_fusion = f32[1,4,1240,512]{3,2,1,0:T(8,128)} fusion(bf16[4,1248,512]{2,1,0:T(8,128)(2,1)S(1)} %bitcast.60), kind=kLoop, calls=%fused_computation | loop fusion | flops 2539520 | bytes 15237120 | tf_op jit(solution)/shard_map/convert_element_type | solution.py:857
  (32 shorter events, 3.2 us)
Async XLA Ops:
  443.2 4.6 %copy-start = (bf16[896,3072]{1,0:T(8,128)(2,1)S(1)}, bf16[896,3072]{1,0:T(8,128)(2,1)}, u32[]{:S(2)}) copy-start(bf16[896,3072]{1,0:T(8,128)(2,1)} %get-tuple-element.11) | copy-start | bytes 16515076
  448.0 5.9 %slice-start = ((s8[5111808]{0:T(1024)(128)(4,1)}), s8[4194304]{0:T(1024)(128)(4,1)S(1)}, s32[]{:S(2)}) async-start(s8[5111808]{0:T(1024)(128)(4,1)} %bitcast.59), calls=%async_computation | async-start | bytes 8388608
  448.0 5.8 %slice-start.1 = ((s8[5111808]{0:T(1024)(128)(4,1)}), s8[917504]{0:T(1024)(128)(4,1)S(1)}, s32[]{:S(2)}) async-start(s8[5111808]{0:T(1024)(128)(4,1)} %bitcast.59), calls=%async_computation.1 | async-start | bytes 1835008

commit v3 on v2

--- a/solution.py
+++ b/solution.py
@@ -13,6 +13,8 @@
 F32 = jnp.float32
 MESH = pl.DeviceIdType.MESH
 TILE = 256
+WIDE = 512
+DEEP = 1536
 
 HALVES = (
     {"first": 0, "rows": 592, "deep": 640, "starts": (0, 192, 384), "win": 208, "wide": 256, "out": 592},
@@ -57,12 +59,17 @@
         body(rows - rows % step, rows % step)
 
 
-def over_tiles(count, body):
+def over_tiles(count, body, size=TILE, together=1):
     def one(index, carry):
-        body(pl.multiple_of(index * TILE, TILE))
+        for k in range(together):
+            body(pl.multiple_of(index * (size * together) + k * size, size))
         return carry
 
-    lax.fori_loop(0, count, one, 0)
+    if count == together:
+        for k in range(together):
+            body(k * size)
+    else:
+        lax.fori_loop(0, count // together, one, 0)
 
 
 def fold8(values):
@@ -137,11 +144,11 @@
     rows, gate = HALVES[half]["rows"], w.narrow.shape[0]
 
     def body(at):
-        active, slope = gelu_tile(w, rows, pl.multiple_of(gate + at, TILE))
+        active, slope = gelu_tile(w, rows, gate + at)
         w.wide[0:rows, pl.ds(at, TILE)] = active
-        w.gh[0:rows, pl.ds(pl.multiple_of(gate + at, TILE), TILE)] = slope.astype(BF)
-
-    over_tiles(gate // TILE, body)
+        w.gh[0:rows, pl.ds(gate + at, TILE)] = slope.astype(BF)
+
+    over_tiles(gate // TILE, body, TILE, 6)
 
 
 def gate_norm(w, half):
@@ -166,7 +173,7 @@
         w.u[0:rows, pl.ds(at, TILE)] = active.astype(BF)
         w.gh[0:rows, pl.ds(at, TILE)] = slope.astype(BF)
 
-    over_tiles(gate // TILE, body)
+    over_tiles(gate // TILE, body, TILE, 6)
 
 
 def mix(w, half):
@@ -185,18 +192,18 @@
         w.s[0:rows, span] = mixed.astype(BF)
         w.m[0:rows, span] = (w.u[0:rows, span].astype(F32) * mixed).astype(BF)
 
-    over_tiles(gate // TILE, body)
+    over_tiles(gate // TILE, body, TILE, 6)
 
 
 def project(w, half, x_at, keep):
     rows = HALVES[half]["rows"]
 
     def body(at):
-        span = pl.ds(at, TILE)
+        span = pl.ds(at, WIDE)
         y = dot(w.m[0:rows, :], w.narrow[:, span])
         keep(span, x_at(0, rows, span).astype(F32) + (y + w.ob[:, span]))
 
-    over_tiles(w.narrow.shape[1] // TILE, body)
+    over_tiles(w.narrow.shape[1] // WIDE, body, WIDE)
 
 
 def cotangent(w, half, gy_at):
@@ -221,10 +228,10 @@
     deep = HALVES[half]["deep"]
 
     def body(at):
-        span = pl.ds(at, TILE)
+        span = pl.ds(at, DEEP)
         w.ng[:, span] += dot(w.gt[:, 0:deep], w.m[0:deep, span])
 
-    over_tiles(w.narrow.shape[0] // TILE, body)
+    over_tiles(w.narrow.shape[0] // DEEP, body, DEEP)
 
 
 def split(w, half):
@@ -232,16 +239,16 @@
     line = (w.pa, w.pb)[half]
 
     def body(at):
-        span = pl.ds(at, TILE)
+        span = pl.ds(at, DEEP)
         gm = dot_nt(w.g[0:rows, :], w.narrow[span, :])
         moved = (gm * w.u[0:rows, span].astype(F32)).astype(BF)
         mixed = w.s[0:rows, span].astype(F32)
         w.s[0:rows, span] = moved
         moved = moved.astype(F32)
-        line[...] += moved[:, 0:128] + moved[:, 128:256]
+        line[...] += sum(moved[:, i : i + 128] for i in range(0, DEEP, 128))
         w.gh[0:rows, span] = (gm * mixed * w.gh[0:rows, span].astype(F32)).astype(BF)
 
-    over_tiles(w.narrow.shape[0] // TILE, body)
+    over_tiles(w.narrow.shape[0] // DEEP, body, DEEP)
 
 
 def unmix(w, half):
@@ -256,7 +263,7 @@
         ]
         w.wide[0 : spec["rows"], span] = assemble(parts, spec["starts"], spec["rows"])
 
-    over_tiles(w.narrow.shape[0] // TILE, body)
+    over_tiles(w.narrow.shape[0] // TILE, body, TILE, 6)
 
 
 def spatial_total(w, half):
@@ -288,19 +295,19 @@
     deep = HALVES[half]["deep"]
 
     def body(at):
-        span = pl.ds(at, TILE)
+        span = pl.ds(at, DEEP)
         w.wg[:, span] += dot(w.nt[:, 0:deep], w.gh[0:deep, span])
 
-    over_tiles(w.widen.shape[1] // TILE, body)
+    over_tiles(w.widen.shape[1] // DEEP, body, DEEP)
 
 
 def pull(w, half):
     rows = HALVES[half]["rows"]
 
     def body(at):
-        w.wide[0:rows, pl.ds(at, TILE)] = dot_nt(w.gh[0:rows, :], w.widen[pl.ds(at, TILE), :])
-
-    over_tiles(w.widen.shape[0] // TILE, body)
+        w.wide[0:rows, pl.ds(at, WIDE)] = dot_nt(w.gh[0:rows, :], w.widen[pl.ds(at, WIDE), :])
+
+    over_tiles(w.widen.shape[0] // WIDE, body, WIDE)
 
 
 def entry_back(w, half, x_at, gy_at, keep):
@@ -487,21 +494,20 @@
         total = w.gh[rows, columns].astype(F32) + land[row : row + size, :].astype(F32)
         w.gh[rows, columns] = total.astype(BF)
 
-    for chunk in range(CHUNKS):
-        for side in range(2):
-            halves(chunk, side).start()
-    for chunk in range(CHUNKS):
+    def by_core(chunk):
         for side in range(2):
             halves(chunk, side).wait_recv()
             accumulate(rows_at(group.core, chunk, 0), side, 2 * chunk * part, 2 * part)
             quarters(chunk, side).start()
-    for chunk in range(CHUNKS):
+
+    def by_x(chunk):
         for side in range(2):
             quarters(chunk, side).wait_recv()
             accumulate(rows_at(group.core, chunk, group.x), side, PACKED // 2 + chunk * part, part)
         for k in range(3):
             shares(chunk, k).start()
-    for chunk in range(CHUNKS):
+
+    def by_z(chunk):
         total = w.gh[pl.ds(rows_at(group.core, chunk, group.x), part), column_of(group.z)].astype(F32)
         for k in range(3):
             shares(chunk, k).wait_recv()
@@ -510,14 +516,26 @@
         own(chunk).start()
         for k in range(3):
             back_around(chunk, k).start()
-    for chunk in range(CHUNKS):
+
+    def give_x(chunk):
         own(chunk).wait()
         for k in range(3):
             back_around(chunk, k).wait_recv()
         back_across(chunk).start()
-    for chunk in range(CHUNKS):
+
+    def give_core(chunk):
         back_across(chunk).wait_recv()
         back_beside(chunk).start()
+
+    for chunk in range(CHUNKS):
+        for side in range(2):
+            halves(chunk, side).start()
+    stages = (by_core, by_x, by_z, give_x, give_core)
+    lags = (0, 1, 2, 3, 4)
+    for turn_at in range(CHUNKS + lags[-1]):
+        for stage, lag in zip(stages, lags):
+            if 0 <= turn_at - lag < CHUNKS:
+                stage(turn_at - lag)
     for chunk in range(CHUNKS):
         back_beside(chunk).wait_recv()
     for chunk in range(CHUNKS):

time: 460 us -> 413 us (0.90)
  Pallas kernels: 415 us -> 365 us
    pallas_call x1, Pallas kernels: 415 us -> 365 us  [shards(): pl.pallas_call(layer_kernel, out_shape=outputs_of(micro, width, hidden),...]
where the time goes in v3:
time: 413 us; the launch traced here: 409 us
  Pallas kernels  365 us (88%)
  local copies, waits for them, and re-layouts  20.5 us (5%)
  other arithmetic  16.4 us (4%)
  between operations  7.45 us (2%)
    pallas_call x1, Pallas kernels, shards(): pl.pallas_call(layer_kernel, out_shape=outputs_of(micro, width, hidden),...  365 us

profile of v3, /device:TPU:0, one launch (start us, length us, event | category | flops | bytes accessed | tf_op | source)
XLA Modules:
  0.0 409.3 jit_solution(7716403234706714822)
XLA Ops:
  0.6 1.3 fusion.7
  8.4 0.8 fusion.5
  9.2 0.8 constant_dynamic-slice_fusion
  9.9 0.7 reduce
  10.8 0.9 constant_dynamic-slice_fusion.3
  11.8 1.0 constant_dynamic-slice_fusion.2
  13.0 1.1 copy.29
  14.1 0.9 broadcast_in_dim.26.refs_7_
  15.1 0.8 pad_maximum_fusion.3.refs_5_
  15.9 0.9 broadcast_in_dim.27.refs_8_
  17.0 0.9 copy.30.refs_3_
  18.1 0.8 pad_maximum_fusion.1.refs_6_
  19.2 1.0 copy.31.refs_4_
  20.2 5.2 %pad.66.refs_0_ = bf16[4,1248,512]{2,1,0:T(8,128)(2,1)} pad(bf16[4,1240,512]{2,1,0:T(8,128)(2,1)} %bitcast.58, bf16[]{:T(256)} %constant.14.clone.1), padding=0_0x0_8x0_0 | pad | bytes 10190850 | tf_op jit(solution)/shard_map/jit(_pad)/pad | solution.py:803
  25.5 365.0 %layer_relay.1 = (bf16[4,1248,512]{2,1,0:T(8,128)(2,1)}, bf16[896,3072]{1,0:T(8,128)(2,1)}) custom-call(bf16[4,1248,512]{2,1,0:T(8,128)(2,1)} %pad.66.refs_0_, bf16[512,3072]{1,0:T(8,128)(2,1)} %bitcast.61, bf16[1536,512]{1,0:T(8,128)(2,1)} %bitcast.64, bf16[3,208,256]{2,1,0:T(8,128)(2,1)} %copy.30.refs_3_, bf16[2,336,384]{2,1,0:T(8,128)(2,1)} %copy.31.refs_4_, ...), custom_call_target="tpu_custom_call" | custom-call | tf_op jit(solution)/shard_map/layer_relay/pallas_call | solution.py:818
  390.5 0.8 slice_convert_fusion
  391.9 0.6 slice_reduce_fusion
  392.5 0.6 broadcast_in_dim_reshape_squeeze.7
  393.1 1.3 fusion.6
  395.8 0.7 fusion.1
  396.4 1.3 copy.33
  397.9 3.7 bitcast_convert_fusion.1
  401.6 2.1 convert_element_type.61
  403.7 5.4 %bitcast_convert_fusion = f32[1,4,1240,512]{3,2,1,0:T(8,128)} fusion(bf16[4,1248,512]{2,1,0:T(8,128)(2,1)S(1)} %bitcast.60), kind=kLoop, calls=%fused_computation | loop fusion | flops 2539520 | bytes 15237120 | tf_op jit(solution)/shard_map/convert_element_type | solution.py:875
  (32 shorter events, 3.2 us)
Async XLA Ops:
  393.1 4.6 %copy-start = (bf16[896,3072]{1,0:T(8,128)(2,1)S(1)}, bf16[896,3072]{1,0:T(8,128)(2,1)}, u32[]{:S(2)}) copy-start(bf16[896,3072]{1,0:T(8,128)(2,1)} %get-tuple-element.11) | copy-start | bytes 16515076
  397.8 5.9 %slice-start = ((s8[5111808]{0:T(1024)(128)(4,1)}), s8[4194304]{0:T(1024)(128)(4,1)S(1)}, s32[]{:S(2)}) async-start(s8[5111808]{0:T(1024)(128)(4,1)} %bitcast.59), calls=%async_computation | async-start | bytes 8388608
  397.9 5.8 %slice-start.1 = ((s8[5111808]{0:T(1024)(128)(4,1)}), s8[917504]{0:T(1024)(128)(4,1)S(1)}, s32[]{:S(2)}) async-start(s8[5111808]{0:T(1024)(128)(4,1)} %bitcast.59), calls=%async_computation.1 | async-start | bytes 1835008

commit v4 on v3

--- a/solution.py
+++ b/solution.py
@@ -103,12 +103,14 @@
     "bnd", "widen", "narrow", "sp_a", "sp_b", "spt_a", "spt_b", "pos_a", "pos_b",
     "eg", "es", "hb", "gg", "gs", "ob",
 )
-OUTPUTS = ("res", "packed")
+OUTPUTS = ("res", "packed", "saved_u", "saved_z", "saved_upper", "saved_lower")
+SAVED = ("u", "z", "upper", "lower")
 SCRATCH = (
     "wg", "ng", "ga", "gb", "pa", "pb", "gate_sum", "entry_sum",
     "buf", "n", "nt", "g", "gt", "u", "s", "m", "q", "z", "wide", "gh",
     "stage", "kept", "load_sem", "send_sem", "recv_sem", "out_sem",
     "ready", "across_send", "across_recv", "around_send", "around_recv", "own_sem",
+    "save_sem", "fetch_sem",
 )
 
 
@@ -161,6 +163,14 @@
         w.z[span, :] = z.astype(BF)
         w.q[span, :] = (z * w.gg[...] + w.gs[...]).astype(BF)
         w.gh[span, gate:] = (w.gh[span, gate:].astype(F32) * factor).astype(BF)
+
+    over_rows(HALVES[half]["rows"], 336, body, PART)
+
+
+def gate_again(w, half):
+    def body(at, size):
+        span = pl.ds(at, size)
+        w.q[span, :] = (w.z[span, :].astype(F32) * w.gg[...] + w.gs[...]).astype(BF)
 
     over_rows(HALVES[half]["rows"], 336, body, PART)
 
@@ -604,22 +614,73 @@
 
         return read
 
+    def saved(name, index, half):
+        span = pl.ds(0, HALVES[half]["rows"])
+        gate = w.narrow.shape[0]
+        here = {
+            "u": w.u.at[span],
+            "z": w.z.at[span],
+            "upper": w.gh.at[span, pl.ds(0, gate)],
+            "lower": w.gh.at[span, pl.ds(gate, gate)],
+        }
+        return here[name], getattr(w, "saved_" + name).at[index, half, span]
+
+    def save(name, index, half):
+        here, there = saved(name, index, half)
+        return pltpu.make_async_copy(here, there, w.save_sem.at[SAVED.index(name)])
+
+    def fetch(name, index, half):
+        here, there = saved(name, index, half)
+        return pltpu.make_async_copy(there, here, w.fetch_sem.at[SAVED.index(name)])
+
+    def before(index, half):
+        return (index, 0) if half == 1 else (index - 1, 1)
+
     def forward(step, index, half):
         rows = HALVES[half]["rows"]
         x_at = rows_of(section, index, half)
+        saves = is_first if half == 1 else jnp.logical_and(is_first, index > 0)
+
+        def free(*names):
+            @pl.when(saves)
+            def _():
+                for name in names:
+                    save(name, *before(index, half)).wait()
+
+        def put_away(*names):
+            @pl.when(is_first)
+            def _():
+                for name in names:
+                    save(name, index, half).start()
+
         entry_norm(w, half, x_at)
-        lower_half(w, half)
-        gate_norm(w, half)
-        upper_half(w, half)
-        mix(w, half)
 
         @pl.when(step < micro)
         def _():
-            @pl.when(jnp.logical_and(is_second, step > 0))
+            free("lower")
+            lower_half(w, half)
+            free("z")
+            gate_norm(w, half)
+            put_away("z", "lower")
+            free("u", "upper")
+            upper_half(w, half)
+            put_away("u", "upper")
+
+        @pl.when(step >= micro)
+        def _():
+            fetch("z", index, half).wait()
+            gate_again(w, half)
+            fetch("u", index, half).wait()
+
+        mix(w, half)
+
+        @pl.when(step < micro)
+        def _():
+            @pl.when(jnp.logical_and(is_second, index > 0))
             def _():
                 store(index - 1, half).wait()
 
-            @pl.when(jnp.logical_and(is_first, step > 0))
+            @pl.when(jnp.logical_and(is_first, index > 0))
             def _():
                 send(index - 1, half).wait_send()
 
@@ -645,14 +706,34 @@
     def backward(step, index, half):
         x_at = rows_of(section, index, half)
         gy_at = rows_of(1 - section, index, half)
+
+        def need(*names):
+            @pl.when(is_first)
+            def _():
+                for name in names:
+                    fetch(name, index, half).wait()
+
+        def done(*names):
+            more = is_first if half == 0 else jnp.logical_and(is_first, index < micro - 1)
+
+            @pl.when(more)
+            def _():
+                for name in names:
+                    fetch(name, *((index, 1) if half == 0 else (index + 1, 0))).start()
+
         cotangent(w, half, gy_at)
         narrow_total(w, half)
+        need("upper")
         split(w, half)
+        done("u")
         unmix(w, half)
         spatial_total(w, half)
+        need("lower")
         gate_back(w, half)
+        done("z")
         widen_total(w, half)
         pull(w, half)
+        done("upper", "lower")
 
         @pl.when(is_first)
         def _():
@@ -680,24 +761,31 @@
 
     def one_step(step, carry):
         index = lax.rem(step, micro)
+
+        @pl.when(jnp.logical_and(is_first, step == micro))
+        def _():
+            for name in SAVED:
+                save(name, micro - 1, 1).wait()
+                fetch(name, 0, 0).start()
+
         for half in range(2):
 
             @pl.when(step < micro)
             def _():
                 load(index, half).wait()
 
-            @pl.when(is_second)
-            def _():
-                send(index, half).wait_recv()
+                @pl.when(is_second)
+                def _():
+                    send(index, half).wait_recv()
 
             forward(step, index, half)
 
-            @pl.when(jnp.logical_and(is_first, step >= micro))
-            def _():
-                send(index, half).wait_recv()
-
             @pl.when(jnp.logical_or(is_second, step >= micro))
             def _():
+                @pl.when(is_first)
+                def _():
+                    send(index, half).wait_recv()
+
                 backward(step, index, half)
 
         return carry
@@ -756,6 +844,8 @@
         pltpu.SemaphoreType.DMA((2, 3, CHUNKS)),
         pltpu.SemaphoreType.DMA((2, 3, CHUNKS)),
         pltpu.SemaphoreType.DMA((CHUNKS,)),
+        pltpu.SemaphoreType.DMA((len(SAVED),)),
+        pltpu.SemaphoreType.DMA((len(SAVED),)),
     ]
 
 
@@ -763,6 +853,7 @@
     return (
         jax.ShapeDtypeStruct((micro, PADDED, width), BF),
         jax.ShapeDtypeStruct((PACKED, hidden), BF),
+        *[jax.ShapeDtypeStruct((micro, 2, HALVES[1]["rows"], hidden // 2), BF)] * len(SAVED),
     )
 
 
@@ -819,7 +910,7 @@
         layer_kernel,
         out_shape=outputs_of(micro, width, hidden),
         in_specs=[anywhere] + [vmem] * 14,
-        out_specs=[anywhere] * 2,
+        out_specs=[anywhere] * len(OUTPUTS),
         scratch_shapes=scratch_of(micro, width, hidden),
         compiler_params=pltpu.CompilerParams(
             collective_id=0, has_side_effects=True, vmem_limit_bytes=int(63.9 * 2**20)
@@ -842,7 +933,7 @@
         gate_shift,
         output_bias,
     )
-    results, packed = outs
+    results, packed = outs[:2]
     if lax.axis_size("dp") != 16:
         packed = lax.psum(packed.astype(F32), "dp").astype(BF)
     widen_grad = packed[:width].astype(F32)

time: 413 us -> 468 us (1.13)
  Pallas kernels: 365 us -> 418 us
    pallas_call x1, Pallas kernels: 365 us -> 418 us  [shards(): pl.pallas_call(layer_kernel, out_shape=outputs_of(micro, width, hidden),...]
where the time goes in v4:
time: 468 us; the launch traced here: 463 us
  Pallas kernels  418 us (89%)
  local copies, waits for them, and re-layouts  20.5 us (4%)
  other arithmetic  16.4 us (4%)
  between operations  7.82 us (2%)
    pallas_call x1, Pallas kernels, shards(): pl.pallas_call(layer_kernel, out_shape=outputs_of(micro, width, hidden),...  418 us

profile of v4, /device:TPU:0, one launch (start us, length us, event | category | flops | bytes accessed | tf_op | source)
XLA Modules:
  0.0 462.9 jit_solution(12800674464232784284)
XLA Ops:
  0.6 1.3 fusion.7
  8.4 0.8 fusion.5
  9.2 0.8 constant_dynamic-slice_fusion
  9.9 0.7 reduce
  10.8 0.9 constant_dynamic-slice_fusion.3
  11.8 1.0 constant_dynamic-slice_fusion.2
  13.0 1.1 copy.29
  14.1 0.9 broadcast_in_dim.26.refs_7_
  15.1 0.8 pad_maximum_fusion.3.refs_5_
  15.9 0.9 broadcast_in_dim.27.refs_8_
  17.0 0.9 copy.30.refs_3_
  18.1 0.8 pad_maximum_fusion.1.refs_6_
  19.2 1.0 copy.31.refs_4_
  20.2 5.2 %pad.66.refs_0_ = bf16[4,1248,512]{2,1,0:T(8,128)(2,1)} pad(bf16[4,1240,512]{2,1,0:T(8,128)(2,1)} %bitcast.58, bf16[]{:T(256)} %constant.14.clone.1), padding=0_0x0_8x0_0 | pad | bytes 10190850 | tf_op jit(solution)/shard_map/jit(_pad)/pad | solution.py:894
  25.5 418.2 %layer_relay.1 = (bf16[4,1248,512]{2,1,0:T(8,128)(2,1)}, bf16[896,3072]{1,0:T(8,128)(2,1)}, bf16[4,2,656,1536]{3,2,1,0:T(8,128)(2,1)}, bf16[4,2,656,1536]{3,2,1,...) custom-call(bf16[4,1248,512]{2,1,0:T(8,128)(2,1)} %pad.66.refs_0_, ...), custom_call_target="tpu_custom_call" | custom-call | tf_op jit(solution)/shard_map/layer_relay/pallas_call | solution.py:909
  443.7 0.8 slice_convert_fusion
  445.1 0.6 slice_reduce_fusion
  445.7 0.6 broadcast_in_dim_reshape_squeeze.7
  446.3 1.3 fusion.6
  448.9 0.7 fusion.1
  449.6 1.3 copy.33
  451.1 3.7 bitcast_convert_fusion.1
  454.8 2.1 convert_element_type.61
  456.9 5.4 %bitcast_convert_fusion = f32[1,4,1240,512]{3,2,1,0:T(8,128)} fusion(bf16[4,1248,512]{2,1,0:T(8,128)(2,1)S(1)} %bitcast.60), kind=kLoop, calls=%fused_computation | loop fusion | flops 2539520 | bytes 15237120 | tf_op jit(solution)/shard_map/convert_element_type | solution.py:966
  (32 shorter events, 3.2 us)
Async XLA Ops:
  446.3 4.6 copy-start
  451.0 5.9 %slice-start = ((s8[5111808]{0:T(1024)(128)(4,1)}), s8[4194304]{0:T(1024)(128)(4,1)S(1)}, s32[]{:S(2)}) async-start(s8[5111808]{0:T(1024)(128)(4,1)} %bitcast.59), calls=%async_computation | async-start | bytes 8388608
  451.1 5.8 %slice-start.1 = ((s8[5111808]{0:T(1024)(128)(4,1)}), s8[917504]{0:T(1024)(128)(4,1)S(1)}, s32[]{:S(2)}) async-start(s8[5111808]{0:T(1024)(128)(4,1)} %bitcast.59), calls=%async_computation.1 | async-start | bytes 1835008
